TPU v7x, 32 devices: a whole 2x2x4 slice. The times are simulated.
32 devices in a mesh: section: 2 (over core), dp: 4 (over z), tensor: 4 (over y, x).
Axes of the slice: x: 2, y: 2, z: 4, core: 2. Of those that a mesh axis runs over, the one named last changes fastest.
Arguments:
- text_in: bfloat16 [2, 4096, 768], P(None, ('dp', 'tensor')), may hold values from -6 to 6
- layout_in: bfloat16 [2, 4096, 192], P(None, ('dp', 'tensor')), may hold values from -6 to 6
- text_cot: bfloat16 [2, 4096, 768], P(None, ('dp', 'tensor')), may hold values from -6 to 6
- layout_cot: bfloat16 [2, 4096, 192], P(None, ('dp', 'tensor')), may hold values from -6 to 6
- lengths: int32 [2, 8], P(None, 'dp'), may hold values from 96 to 512, as said below
- text_attend: bfloat16 [2, 768, 3, 768], P('section', None, None, 'tensor'), may hold values from -0.21875 to 0.21875
- text_biases: bfloat16 [2, 2, 768], P('section', None, 'tensor'), may hold values from -1.796875 to 1.796875
- text_output: bfloat16 [2, 768, 768], P('section', None, 'tensor'), may hold values from -0.875 to 0.875
- text_expand: bfloat16 [2, 768, 3072], P('section', None, 'tensor'), may hold values from -0.21875 to 0.21875
- text_offset: bfloat16 [2, 3072], P('section', 'tensor'), may hold values from -1.796875 to 1.796875
- text_shrink: bfloat16 [2, 768, 3072], P('section', None, 'tensor'), may hold values from -0.109375 to 0.109375
- text_vectors: bfloat16 [2, 6, 768], P('section'), may hold values from -1.5 to 1.5, as said below
- layout_attend: bfloat16 [2, 192, 3, 192], P('section', None, None, 'tensor'), may hold values from -0.4375 to 0.4375
- layout_biases: bfloat16 [2, 2, 192], P('section', None, 'tensor'), may hold values from -1.796875 to 1.796875
- layout_output: bfloat16 [2, 192, 192], P('section', None, 'tensor'), may hold values from -1.75 to 1.75
- layout_expand: bfloat16 [2, 192, 768], P('section', None, 'tensor'), may hold values from -0.4375 to 0.4375
- layout_offset: bfloat16 [2, 768], P('section', 'tensor'), may hold values from -1.796875 to 1.796875
- layout_shrink: bfloat16 [2, 192, 768], P('section', None, 'tensor'), may hold values from -0.21875 to 0.21875
- layout_vectors: bfloat16 [2, 6, 192], P('section'), may hold values from -1.5 to 1.5, as said below
Outputs:
- text_out: bfloat16 [2, 2, 4096, 768], P('section', None, ('dp', 'tensor'))
- layout_out: bfloat16 [2, 2, 4096, 192], P('section', None, ('dp', 'tensor'))
- text_back: bfloat16 [2, 2, 4096, 768], P('section', None, ('dp', 'tensor'))
- layout_back: bfloat16 [2, 2, 4096, 192], P('section', None, ('dp', 'tensor'))
- text_attend_grad: float32 [2, 768, 3, 768], P('section', 'dp', None, 'tensor')
- text_biases_grad: float32 [2, 2, 768], P('section', None, 'tensor')
- text_output_grad: float32 [2, 768, 768], P('section', 'dp', 'tensor')
- text_expand_grad: float32 [2, 768, 3072], P('section', 'dp', 'tensor')
- text_offset_grad: float32 [2, 3072], P('section', 'tensor')
- text_shrink_grad: float32 [2, 768, 3072], P('section', 'dp', 'tensor')
- text_vectors_grad: float32 [2, 6, 768], P('section')
- layout_attend_grad: float32 [2, 192, 3, 192], P('section', 'dp', None, 'tensor')
- layout_biases_grad: float32 [2, 2, 192], P('section', None, 'tensor')
- layout_output_grad: float32 [2, 192, 192], P('section', 'dp', 'tensor')
- layout_expand_grad: float32 [2, 192, 768], P('section', 'dp', 'tensor')
- layout_offset_grad: float32 [2, 768], P('section', 'tensor')
- layout_shrink_grad: float32 [2, 192, 768], P('section', 'dp', 'tensor')
- layout_vectors_grad: float32 [2, 6, 192], P('section')
Inputs may be any that keep to these rules, and one draw needn't show every extreme that they name: `lengths`: keys at or past a page's length are padding; some page has exactly 512 tokens. `text_vectors`: rows 1 and 4 are norm gains, the others biases. `layout_vectors`: rows 1 and 4 are norm gains, the others biases.
All inputs are finite; a program needn't handle non-finite values.
Results may differ from a plain program's by a relative error of at most 0.04.
Values may be sent and summed in bfloat16 or wider, within the bound.
A program may use at most 256 MiB of HBM per device.

v0:
```python
import functools
import math

import jax
import jax.numpy as jnp
from jax import lax
from jax.experimental import pallas as pl
from jax.experimental.pallas import tpu as pltpu
from jax.sharding import PartitionSpec as P

HEAD = 64
LHEAD = 16
MESH = pl.DeviceIdType.MESH
bf16 = jnp.bfloat16
f32 = jnp.float32
norm_epsilon = 1e-05
masked_score = -1e30
LANES = 128
SMALL = 1024
STEPS = 12


def mm(left, right, left_axis, right_axis):
    return lax.dot_general(
        left, right, (((left_axis,), (right_axis,)), ((), ())), preferred_element_type=f32
    )


def flip(index, bit):
    return index + bit - 2 * bit * lax.rem(lax.div(index, bit), 2)


def loop(start, stop, body):
    lax.fori_loop(start, stop, lambda i, carry: (body(i), carry)[1], 0)


def at(start, size):
    return pl.ds(pl.multiple_of(start, 16), size)


def lanes_at(start, size):
    return pl.ds(pl.multiple_of(start, LANES), size)


def kernel(
    dp,
    z_inside,
    text_in, lay_in, text_cot, lay_cot, att_t, out_t, exp_t, shr_t, att_l, out_l, exp_l, shr_l,
    bias_t, bias_l, off_t, off_l, vec_t, vec_l, lengths,
    text_out, lay_out, text_back, lay_back, sm_out,
    zs_t, zs_l, zr_t, zr_l, gb_t, gb_l, r1_t, r1_l, r2_t, r2_l, ro_t, ro_l, p_keep,
    w_t, w_l, small, vecs, own_small, own_vec, key_bias, rows_t, rows_l, x_fm, qkv_t, qkv_l, probs,
    ctx_t, ctx_l, xh1, n1b, xh2, act, gp, stats, acc, exs, exr, tmpb, g_fm, dup, dqkv, cols,
    stg_t, stg_l, tv_t, tv_l, fv_t, fv_l, smsg, srec, ssum, szr,
    ag_recv, ag_own, ag_fwd, vec_sem, row_sem, ex_send, ex_recv, out_sem, stg_sem, p_sem,
    s1_send, s1_recv, s2_send, s2_recv, so_send, so_recv, z_send, z_recv, tv_sem, fv_sem, zo_sem,
    sm_send, sm_recv, sz_send, sz_recv, so_sem,
):
    c = lax.axis_index("section")
    d = lax.axis_index("dp")
    t = lax.axis_index("tensor")
    t1, t2 = flip(t, 1), flip(t, 2)
    t3 = flip(t1, 2)
    xb = lax.rem(t, 2)
    zp = lax.rem(d, 2)
    tf = t1 + zp * (t2 - t1)
    td = t2 + zp * (t1 - t2)
    dz = flip(d, 1)
    tw = text_in.shape[2]
    lw = lay_in.shape[1]
    width = tw + lw
    tokens = x_fm.shape[2]
    half = tokens // 2
    quarter = tokens // 4
    hid_t, hid_l = exp_t.shape[1], exp_l.shape[1]
    hs, ls = out_t.shape[0], out_l.shape[0]
    heads = hs // HEAD
    blocks = tokens // LANES
    th, lh = tw // 2, lw // 2
    streams = ((0, tw), (tw, lw))
    z_peers = [lax.rem(d + r, dp) for r in range(1, dp)] if z_inside else [dz]

    def remote(src, dst, send, recv, device):
        return pltpu.make_async_remote_copy(
            src_ref=src, dst_ref=dst, send_sem=send, recv_sem=recv, device_id=device, device_id_type=MESH
        )

    def local_copy(src, dst, sem):
        return pltpu.make_async_copy(src, dst, sem)

    def landed(ref, sem):
        pltpu.make_async_copy(ref, ref, sem).wait()

    def start(copies):
        for copy in copies:
            copy.start()

    def wait(copies):
        for copy in copies:
            copy.wait()

    own_vec[...] = jnp.zeros(own_vec.shape, f32)
    own_vec[0:1, 0:hid_t] = off_t[...].astype(f32)
    own_vec[0:1, hid_t : hid_t + hid_l] = off_l[...].astype(f32)
    own_vec[1:2, 0:hs] = bias_t[0:1].astype(f32)
    own_vec[1:2, 2 * hs : 3 * hs] = bias_t[1:2].astype(f32)
    own_vec[1:2, 3 * hs : 3 * hs + ls] = bias_l[0:1].astype(f32)
    own_vec[1:2, 3 * hs + 2 * ls : 3 * hs + 3 * ls] = bias_l[1:2].astype(f32)
    own_small[...] = own_vec[...].astype(bf16)
    own_vec[0:6, 0:tw] = vec_t[...].astype(f32)
    own_vec[0:6, tw:width] = vec_l[...].astype(f32)

    barrier = pltpu.get_barrier_semaphore()
    peers = [(1 - c, d, t)] + [(k, d, other) for other in (t1, t2, t3) for k in range(2)] + [(c, z, t) for z in z_peers]
    for peer in peers:
        pl.semaphore_signal(barrier, inc=1, device_id=peer, device_id_type=MESH)
    pl.semaphore_wait(barrier, len(peers))
    other = (1 - c, d, t)

    def row_copies(text, lay, text_to, lay_to, base):
        mine, theirs = xb * half, (1 - xb) * half
        part = c * quarter
        own = [
            local_copy(text.at[xb], text_to.at[at(mine, half)], row_sem.at[base, 0]),
            local_copy(lay.at[xb], lay_to.at[:, lanes_at(mine, half)], row_sem.at[base + 1, 0]),
        ]
        away = [
            remote(
                text.at[1 - xb, at(part, quarter)], text_to.at[at(mine + part, quarter)],
                row_sem.at[base, 1], row_sem.at[base, 2], (c, d, t1),
            ),
            remote(
                lay.at[1 - xb, :, lanes_at(part, quarter)], lay_to.at[:, lanes_at(mine + part, quarter)],
                row_sem.at[base + 1, 1], row_sem.at[base + 1, 2], (c, d, t1),
            ),
        ]
        text_part = text_to.at[at(theirs + part, quarter)]
        lay_part = lay_to.at[:, lanes_at(theirs + part, quarter)]
        across = [
            remote(text_part, text_part, row_sem.at[base, 3], row_sem.at[base, 4], other),
            remote(lay_part, lay_part, row_sem.at[base + 1, 3], row_sem.at[base + 1, 4], other),
        ]
        return own, away, across

    cot_t = fv_t.at[0, pl.ds(0, tokens)]
    in_rows = row_copies(text_in, lay_in, rows_t, x_fm.at[0, pl.ds(tw, lw)], 0)
    cot_rows = row_copies(text_cot, lay_cot, cot_t, g_fm.at[pl.ds(tw, lw)], 2)

    def rows_begin(copies):
        own, away, across = copies
        start(away + own)

    def rows_cross(copies):
        own, away, across = copies
        wait(away)
        start(across)

    def rows_arrive(copies):
        own, away, across = copies
        wait(own + across)

    rows_begin(in_rows)

    text_sources = [att_t.at[pl.ds(j * hs, hs)] for j in range(3)] + [out_t]
    text_sources += [exp_t.at[pl.ds(j * hs, hs)] for j in range(4)] + [shr_t.at[pl.ds(j * hs, hs)] for j in range(4)]
    lay_sources = {12: att_l, 13: out_l, 14: exp_l, 15: shr_l}
    lay_places = {12: (0, 0, 3 * ls), 13: (0, 3 * ls, ls), 14: (1, 0, lw), 15: (2, 0, lw)}
    riders = {0: [12, 16], 3: [13], 4: [14], 8: [15]}

    def source(p):
        if p < STEPS:
            return text_sources[p]
        return lay_sources[p] if p < 16 else own_small

    def place(layer, slot, p):
        if p < STEPS:
            return w_t.at[layer, slot, p // 4, pl.ds((p % 4) * hs, hs)]
        if p < 16:
            which, first, size = lay_places[p]
            return w_l.at[layer, slot, which, pl.ds(first, size)]
        return small.at[layer, slot]

    def pieces(j):
        return [j] + riders.get(j, [])

    all_pieces = [p for j in range(STEPS) for p in pieces(j)]

    def own_first(p):
        return remote(
            source(p), place(c, 1 - zp, p), ag_own.at[p, 0], ag_recv.at[c, 1 - zp, p], (zp, d, tf)
        )

    def own_core(p):
        return remote(source(p), place(1, 0, p), ag_own.at[p, 1], ag_recv.at[1, 0, p], (0, d, t))

    def own_local(p):
        return local_copy(source(p), place(0, 0, p), ag_recv.at[0, 0, p])

    def forwards(layer, p):
        return [
            remote(
                place(layer, 1 - zp, p), place(layer, 1, p),
                ag_fwd.at[layer, p, 0], ag_recv.at[layer, 1, p], (1, d, td),
            ),
            remote(
                place(layer, 1 - zp, p), place(layer, 1 - zp, p),
                ag_fwd.at[layer, p, 1], ag_recv.at[layer, 1 - zp, p], (zp, dz, t),
            ),
        ]

    def fw(layer, *steps):
        @pl.when(c == zp)
        def _():
            for j in steps:
                for p in pieces(j):
                    landed(place(layer, 1 - zp, p), ag_recv.at[layer, 1 - zp, p])
                    start(forwards(layer, p))

    def need(layer, *steps):
        for j in steps:
            for p in pieces(j):
                landed(place(layer, zp, p), ag_recv.at[layer, zp, p])

        @pl.when(c != zp)
        def _():
            for j in steps:
                for p in pieces(j):
                    landed(place(layer, 1 - zp, p), ag_recv.at[layer, 1 - zp, p])

    vec_copies = [
        local_copy(own_vec, vecs.at[c], vec_sem.at[0]),
        remote(own_vec, vecs.at[c], vec_sem.at[1], vec_sem.at[2], other),
    ]
    start(vec_copies)

    @pl.when(c == 0)
    def _():
        for p in all_pieces:
            start([own_first(p), own_local(p)])

    @pl.when(c == 1)
    def _():
        start([own_core(p) for p in all_pieces])

    def start_second_layer():
        @pl.when(c == 1)
        def _():
            start([own_first(p) for p in all_pieces])

    page_len = lengths[xb, lax.div(t, 2)]
    positions = lax.broadcasted_iota(jnp.int32, key_bias.shape, 0)
    key_bias[...] = jnp.where(positions < page_len, 0.0, masked_score).astype(f32)
    smsg[...] = jnp.zeros(smsg.shape, f32)
    ones = jnp.ones((8, tokens), bf16)
    wait(vec_copies)

    def load_columns(layer):
        for k in range(2):
            cols[k] = small[layer, k].astype(f32).T
        cols[2] = vecs[layer].T

    def column(k, first, size, lane):
        return cols[k, pl.ds(first, size), lane : lane + 1]

    def exchange_copy(n):
        return remote(exs, exr.at[n % 2], ex_send.at[n], ex_recv.at[n], other)

    def exchanged(n, first, size, lanes):
        return exs[pl.ds(first, size), lanes].astype(f32) + exr[n % 2, pl.ds(first, size), lanes].astype(f32)

    def project(layer, s):
        mixed = mm(w_t[layer, s, 0, 0 : 3 * hs], x_fm[layer, 0:tw], 1, 0)
        qkv_t[layer, s] = (mixed + cols[s, 0 : 3 * hs, 1:2]).astype(bf16)
        mixed = mm(w_l[layer, s, 0, 0 : 3 * ls], x_fm[layer, tw:width], 1, 0)
        qkv_l[layer, s] = (mixed + cols[s, 3 * hs : 3 * hs + 3 * ls, 1:2]).astype(bf16)

    def head_rows(layer, s, part, h):
        return (
            qkv_t[layer, s, at(part * hs + h * HEAD, HEAD)],
            qkv_l[layer, s, at(part * ls + h * LHEAD, LHEAD)],
        )

    def query(layer, s, h):
        text, lay = head_rows(layer, s, 0, h)
        return jnp.concatenate([text * HEAD**-0.5, lay * LHEAD**-0.5], axis=0).astype(bf16)

    def attend_forward(layer, i):
        s, h = lax.div(i, heads), lax.rem(i, heads)
        keys = jnp.concatenate(head_rows(layer, s, 1, h), axis=0)
        values = jnp.concatenate(head_rows(layer, s, 2, h), axis=0)
        scores = mm(keys, query(layer, s, h), 0, 0) + key_bias[:, 0:1]
        exponent = jnp.exp(scores - jnp.max(scores, axis=0, keepdims=True))
        low = (exponent * (1.0 / jnp.sum(exponent, axis=0, keepdims=True))).astype(bf16)
        probs[i] = low
        context = mm(values, low, 1, 0).astype(bf16)
        ctx_t[layer, s, at(h * HEAD, HEAD)] = context[0:HEAD]
        ctx_l[layer, s, at(h * LHEAD, LHEAD)] = context[HEAD:]

    def attention_partial(layer):
        exs[0:tw] = (
            mm(w_t[layer, 0, 0, 3 * hs : 4 * hs], ctx_t[layer, 0], 0, 0)
            + mm(w_t[layer, 1, 0, 3 * hs : 4 * hs], ctx_t[layer, 1], 0, 0)
        ).astype(bf16)
        exs[tw:width] = (
            mm(w_l[layer, 0, 0, 3 * ls : 4 * ls], ctx_l[layer, 0], 0, 0)
            + mm(w_l[layer, 1, 0, 3 * ls : 4 * ls], ctx_l[layer, 1], 0, 0)
        ).astype(bf16)

    def normalize(hidden):
        center = hidden - jnp.mean(hidden, axis=0, keepdims=True)
        scale = lax.rsqrt(jnp.mean(center * center, axis=0, keepdims=True) + norm_epsilon)
        return center * scale, scale

    def norm_forward(layer, n, which, base, hat_ref, finish):
        def block(b):
            lanes = lanes_at(b * LANES, LANES)
            for k, (first, size) in enumerate(streams):
                hidden = base(first, size, lanes) + exchanged(n, first, size, lanes)
                hat, scale = normalize(hidden + column(2, first, size, 3 * which))
                hat_ref[layer, pl.ds(first, size), lanes] = hat.astype(bf16)
                row = 2 * which + k
                stats[layer, row : row + 1, lanes] = scale
                result = hat * column(2, first, size, 3 * which + 1) + column(2, first, size, 3 * which + 2)
                finish(first, size, lanes, result)

        loop(0, blocks, block)

    def first_norm(layer, n):
        def finish(first, size, lanes, result):
            acc[pl.ds(first, size), lanes] = result
            n1b[layer, pl.ds(first, size), lanes] = result.astype(bf16)

        norm_forward(
            layer, n, 0, lambda s, z, lanes: x_fm[layer, pl.ds(s, z), lanes].astype(f32), xh1, finish
        )

    def second_norm(layer, n, dest):
        def finish(first, size, lanes, result):
            dest[pl.ds(first, size), lanes] = result.astype(bf16)

        norm_forward(layer, n, 1, lambda s, z, lanes: acc[pl.ds(s, z), lanes], xh2, finish)

    def gelu_pair(raised):
        cdf = 0.5 * (1.0 + lax.erf(raised * math.sqrt(0.5)))
        slope = cdf + raised * (jnp.exp(-0.5 * raised * raised) * (1.0 / math.sqrt(2.0 * math.pi)))
        return (raised * cdf).astype(bf16), slope.astype(bf16)

    hb = 256
    per_slot = hid_t // hb

    def expand_block(layer, i):
        s, b = lax.div(i, per_slot), lax.rem(i, per_slot)
        rows = lanes_at(b * hb, hb)
        raised = mm(w_t[layer, s, 1, :, rows], n1b[layer, 0:tw], 0, 0) + cols[s, rows, 0:1]
        act[layer, s, rows], gp[layer, s, rows] = gelu_pair(raised)

    def expand_lay(layer, s):
        raised = mm(w_l[layer, s, 1], n1b[layer, tw:width], 0, 0) + cols[s, hid_t : hid_t + hid_l, 0:1]
        act[layer, s, hid_t:], gp[layer, s, hid_t:] = gelu_pair(raised)

    def shrink_partial(layer):
        exs[0:tw] = (
            mm(w_t[layer, 0, 2], act[layer, 0, 0:hid_t], 1, 0) + mm(w_t[layer, 1, 2], act[layer, 1, 0:hid_t], 1, 0)
        ).astype(bf16)
        exs[tw:width] = (
            mm(w_l[layer, 0, 2], act[layer, 0, hid_t:], 1, 0) + mm(w_l[layer, 1, 2], act[layer, 1, hid_t:], 1, 0)
        ).astype(bf16)

    def rows_out(base, text_to, lay_to):
        mine, theirs = xb * half, (1 - xb) * half
        pairs = (
            (rows_t.at[at(mine, half)], rows_t.at[at(theirs, half)], text_to),
            (rows_l.at[:, lanes_at(mine, half)], rows_l.at[:, lanes_at(theirs, half)], lay_to),
        )
        copies = []
        for k, (own, away, dest) in enumerate(pairs):
            copies.append(local_copy(own, dest.at[xb], out_sem.at[base + k, 0]))
            copies.append(
                remote(away, dest.at[xb], out_sem.at[base + k, 1], out_sem.at[base + k, 2], (c, d, t1))
            )
        return copies

    def send_rows(layer, base, dest_pair, value):
        @pl.when(c == layer)
        def _():
            rows_t[...] = value[0:tw].T
            rows_l[...] = value[tw:width]
            start(rows_out(base, *dest_pair))

    def finish_rows(layer, base, dest_pair):
        @pl.when(c == layer)
        def _():
            wait(rows_out(base, *dest_pair))

    out_pair, back_pair = (text_out, lay_out), (text_back, lay_back)
    rows_cross(in_rows)
    fw(0, 0)
    rows_arrive(in_rows)
    x_fm[0, 0:tw] = rows_t[...].T
    fw(0, 1)
    need(0, 0)
    load_columns(0)

    p_store = local_copy(probs, p_keep, p_sem.at[0])
    p_load = local_copy(p_keep, probs, p_sem.at[1])

    for layer in range(2):
        last = layer == 1
        fw(layer, 2)
        need(layer, 1)
        fw(layer, 3)
        need(layer, 2)
        project(layer, 0)
        fw(layer, 4)
        project(layer, 1)
        if last:
            p_store.wait()
        fw(layer, 5)
        head = functools.partial(attend_forward, layer)
        loop(0, 2, head)
        fw(layer, 6)
        loop(2, 4, head)
        fw(layer, 7)
        loop(4, 6, head)
        if last:
            rows_cross(cot_rows)
        else:
            p_store.start()
            rows_begin(cot_rows)
        need(layer, 3)
        attention_partial(layer)
        swap = exchange_copy(2 * layer)
        swap.start()
        fw(layer, 8)
        swap.wait()
        first_norm(layer, 2 * layer)
        fw(layer, 9)
        need(layer, 4, 5, 6, 7)
        expand = functools.partial(expand_block, layer)
        loop(0, per_slot, expand)
        fw(layer, 10)
        if not last:
            need(layer, 8, 9)
            start_second_layer()
        loop(per_slot, 2 * per_slot, expand)
        fw(layer, 11)
        loop(0, 2, functools.partial(expand_lay, layer))
        if last:
            need(layer, 8, 9, 10, 11)
            rows_arrive(cot_rows)
        else:
            need(layer, 10)
            fw(1, 0)
            need(layer, 11)
        shrink_partial(layer)
        swap = exchange_copy(2 * layer + 1)
        swap.start()
        if not last:
            fw(1, 1)
        else:
            g_fm[0:tw] = cot_t[...].T
        swap.wait()
        if not last:
            second_norm(0, 1, x_fm.at[1])
            send_rows(0, 0, out_pair, x_fm.at[1])
            need(1, 0)
            load_columns(1)
        else:
            second_norm(1, 3, tmpb)
            send_rows(1, 0, out_pair, tmpb)

    def grad_store(layer, chunk, s):
        return [
            local_copy(stg_t.at[s], gb_t.at[layer, chunk, s], stg_sem.at[s, 0]),
            local_copy(stg_l.at[s], gb_l.at[layer, chunk, s], stg_sem.at[s, 1]),
        ]

    def store_grad(layer, chunk, s, text_value, lay_value):
        stg_t[s] = text_value
        stg_l[s] = lay_value
        start(grad_store(layer, chunk, s))

    def first_sends(layer, chunk):
        zero, one = [], []
        for k, (grad, come, total, size) in enumerate(((gb_t, r1_t, r2_t, th), (gb_l, r1_l, r2_l, lh))):
            h1, h2 = pl.ds(0, size), pl.ds(size, size)
            zero.append(
                remote(
                    grad.at[layer, chunk, 1, h1], total.at[chunk, 0, h1],
                    s1_send.at[layer, chunk, k, 0], s2_recv.at[chunk, 0, 0, k], (layer, d, t1),
                )
            )
            one.append(
                remote(
                    grad.at[layer, chunk, 1, h1], come.at[layer, chunk],
                    s1_send.at[layer, chunk, k, 0], s1_recv.at[layer, chunk, k], (1, d, t1),
                )
            )
            one.append(
                remote(
                    grad.at[layer, chunk, 1, h2], come.at[layer, chunk],
                    s1_send.at[layer, chunk, k, 1], s1_recv.at[layer, chunk, k], (0, d, t2),
                )
            )
            one.append(
                remote(
                    grad.at[layer, chunk, 0, h2], total.at[chunk, 1, h2],
                    s1_send.at[layer, chunk, k, 2], s2_recv.at[chunk, 1, 1, k], (layer, d, t2),
                )
            )
        if layer == 1:
            for k, (grad, arrive) in enumerate(((gb_t, ro_t), (gb_l, ro_l))):
                zero.append(
                    remote(
                        grad.at[1, chunk, 0], arrive.at[chunk], so_send.at[chunk, k], so_recv.at[chunk, k], other
                    )
                )
        return zero, one

    def grads_go(layer, chunk):
        for s in range(2):
            wait(grad_store(layer, chunk, s))
        zero, one = first_sends(layer, chunk)

        @pl.when(c == 0)
        def _():
            start(zero)

        @pl.when(c == 1)
        def _():
            start(one)

    tx = t1 + c * (t2 - t1)
    transit_groups = ((gb_t, r1_t, r2_t, th, tv_t), (gb_l, r1_l, r2_l, lh, tv_l))

    def mine(grad, layer, chunk, size):
        return grad.at[layer, chunk, 1 - c, at((1 - c) * size, size)]

    def second_sends(layer, chunk):
        return [
            remote(
                mine(grad, layer, chunk, size), total.at[chunk, c, at((1 - c) * size, size)],
                s2_send.at[layer, chunk, k], s2_recv.at[chunk, c, 1 - c, k], (layer, d, tx),
            )
            for k, (grad, come, total, size, tv) in enumerate(transit_groups)
        ]

    def transit_loads(layer, chunk):
        copies = []
        for k, (grad, come, total, size, tv) in enumerate(transit_groups):
            copies.append(local_copy(mine(grad, layer, chunk, size), tv.at[0], tv_sem.at[k, 0]))
            copies.append(local_copy(come.at[layer, chunk], tv.at[1], tv_sem.at[k, 1]))
        return copies

    def transit_stores(layer, chunk):
        return [
            local_copy(tv.at[0], mine(grad, layer, chunk, size), tv_sem.at[k, 2])
            for k, (grad, come, total, size, tv) in enumerate(transit_groups)
        ]

    def transit_load(layer, chunk):
        for k, (grad, come, total, size, tv) in enumerate(transit_groups):
            landed(come.at[layer, chunk], s1_recv.at[layer, chunk, k])
        start(transit_loads(layer, chunk))

    def transit_add(layer, chunk):
        wait(transit_loads(layer, chunk))
        for tv in (tv_t, tv_l):
            tv[0] = (tv[0].astype(f32) + tv[1].astype(f32)).astype(bf16)
        start(transit_stores(layer, chunk))

    def transit_send(layer, chunk):
        wait(transit_stores(layer, chunk))
        start(second_sends(layer, chunk))

    def transit(layer, chunk):
        transit_load(layer, chunk)
        transit_add(layer, chunk)
        transit_send(layer, chunk)

    parts = dp if z_inside else 2
    final_groups = ((gb_t, ro_t, r2_t, fv_t, zs_t, zr_t), (gb_l, ro_l, r2_l, fv_l, zs_l, zr_l))

    def part_sends(chunk, r):
        copies = []
        for k, (grad, arrive, total, fv, zs, zr) in enumerate(final_groups):
            size = fv.shape[1] // parts
            if not z_inside:
                rows = pl.ds(r * size, size)
                copies.append(local_copy(fv.at[0, rows], zs.at[chunk, rows], zo_sem.at[k, r]))
                continue
            j = lax.rem(d + r, dp)
            piece = fv.at[0, at(j * size, size)]
            if r == 0:
                copies.append(local_copy(piece, zr.at[chunk, 0], zo_sem.at[k, 0]))
            else:
                copies.append(
                    remote(piece, zr.at[chunk, r], z_send.at[chunk, k, r], z_recv.at[chunk, k, r], (c, j, t))
                )
        return copies

    def part_rows(r, size):
        if not z_inside:
            return pl.ds(r * size, size)
        return at(lax.rem(d + r, dp) * size, size)

    def part_loads(layer, chunk, r):
        copies = []
        for k, (grad, arrive, total, fv, zs, zr) in enumerate(final_groups):
            rows = part_rows(r, fv.shape[1] // parts)
            own = arrive.at[chunk, rows] if layer == 1 else grad.at[layer, chunk, 0, rows]
            for i, src in enumerate((own, total.at[chunk, 0, rows], total.at[chunk, 1, rows])):
                copies.append(local_copy(src, fv.at[i, rows], fv_sem.at[k, i, r]))
        return copies

    order = list(range(1, parts)) + [0]

    def sent(copies, inside):
        for copy in copies:
            if inside:
                copy.wait_send()
            else:
                copy.wait()

    def final(layer, chunk, before):
        @pl.when(c == layer)
        def _():
            if before is not None:
                for r in order:
                    sent(part_sends(before, r), z_inside and r > 0)
            for k, (grad, arrive, total, fv, zs, zr) in enumerate(final_groups):
                size = (th, lh)[k]
                for way in range(2):
                    for h in range(2):
                        landed(total.at[chunk, way, pl.ds(h * size, size)], s2_recv.at[chunk, way, h, k])
                if layer == 1:
                    landed(arrive.at[chunk], so_recv.at[chunk, k])
            for r in order:
                start(part_loads(layer, chunk, r))
            for r in order:
                wait(part_loads(layer, chunk, r))
                for grad, arrive, total, fv, zs, zr in final_groups:
                    rows = part_rows(r, fv.shape[1] // parts)
                    summed = fv[0, rows].astype(f32) + fv[1, rows].astype(f32) + fv[2, rows].astype(f32)
                    fv[0, rows] = summed.astype(bf16)
                start(part_sends(chunk, r))

    def small_sends(layer):
        zero = [remote(smsg.at[layer, 1], srec.at[0], sm_send.at[layer, 0], sm_recv.at[0], (layer, d, t1))]
        if layer == 1:
            zero.append(remote(smsg.at[1, 0], srec.at[3], sm_send.at[1, 1], sm_recv.at[3], other))
        one = [
            remote(smsg.at[layer, 0], srec.at[1], sm_send.at[layer, 0], sm_recv.at[1], (layer, d, t2)),
            remote(smsg.at[layer, 1], srec.at[2], sm_send.at[layer, 1], sm_recv.at[2], (layer, d, t3)),
        ]
        return zero, one

    def small_go(layer):
        zero, one = small_sends(layer)

        @pl.when(c == 0)
        def _():
            start(zero)

        @pl.when(c == 1)
        def _():
            start(one)

    def small_z():
        if not z_inside:
            return []
        return [
            remote(ssum, szr.at[r - 1], sz_send.at[r - 1], sz_recv.at[r - 1], (c, lax.rem(d + r, dp), t))
            for r in range(1, dp)
        ]

    def small_total(layer):
        @pl.when(c == layer)
        def _():
            for i in range(3):
                landed(srec.at[i], sm_recv.at[i])
            if layer == 1:
                landed(srec.at[3], sm_recv.at[3])
                own = srec[3]
            else:
                own = smsg[0, 0]
            ssum[...] = own + srec[0] + srec[1] + srec[2]
            start(small_z())

    def row_sums(ref):
        return mm(ones, ref[...], 1, 1)[0:1]

    def vector_sum(layer, row, value):
        for s in range(2):
            smsg[layer, s, 8 + row : 9 + row, 0:width] = value

    def norm_backward(layer, which, hat_ref, incoming):
        def block(b):
            lanes = lanes_at(b * LANES, LANES)
            for k, (first, size) in enumerate(streams):
                grad = incoming(first, size, lanes)
                hat = hat_ref[layer, pl.ds(first, size), lanes].astype(f32)
                row = 2 * which + k
                scale = stats[layer, row : row + 1, lanes]
                gained = grad * column(2, first, size, 3 * which + 1)
                mean_grad = jnp.mean(gained, axis=0, keepdims=True)
                mean_both = jnp.mean(gained * hat, axis=0, keepdims=True)
                result = scale * (gained - mean_grad - hat * mean_both)
                acc[pl.ds(first, size), lanes] = result
                tmpb[pl.ds(first, size), lanes] = result.astype(bf16)
                exs[pl.ds(first, size), lanes] = (grad * hat).astype(bf16)
                g_fm[pl.ds(first, size), lanes] = grad.astype(bf16)

        loop(0, blocks, block)
        vector_sum(layer, 3 * which + 1, row_sums(exs))
        vector_sum(layer, 3 * which + 2, row_sums(g_fm))
        vector_sum(layer, 3 * which, row_sums(tmpb))

    def ffn_backward(layer):
        def text_block(i):
            s, b = lax.div(i, per_slot), lax.rem(i, per_slot)
            rows = lanes_at(b * hb, hb)
            back = mm(w_t[layer, s, 2, :, rows], tmpb[0:tw], 0, 0)
            dup[s, rows] = (back * gp[layer, s, rows].astype(f32)).astype(bf16)

        loop(0, 2 * per_slot, text_block)

        def lay_block(s):
            back = mm(w_l[layer, s, 2], tmpb[tw:width], 0, 0)
            dup[s, hid_t:] = (back * gp[layer, s, hid_t:].astype(f32)).astype(bf16)

        loop(0, 2, lay_block)

    def shrink_grads(layer, s):
        store_grad(
            layer, 2, s,
            mm(tmpb[0:tw], act[layer, s, 0:hid_t], 1, 1).astype(bf16),
            mm(tmpb[tw:width], act[layer, s, hid_t:], 1, 1).astype(bf16),
        )

    def expand_grads(layer, s):
        store_grad(
            layer, 1, s,
            mm(n1b[layer, 0:tw], dup[s, 0:hid_t], 1, 1).astype(bf16),
            mm(n1b[layer, tw:width], dup[s, hid_t:], 1, 1).astype(bf16),
        )

    def expand_partial(layer):
        exs[0:tw] = (
            mm(w_t[layer, 0, 1], dup[0, 0:hid_t], 1, 0) + mm(w_t[layer, 1, 1], dup[1, 0:hid_t], 1, 0)
        ).astype(bf16)
        exs[tw:width] = (
            mm(w_l[layer, 0, 1], dup[0, hid_t:], 1, 0) + mm(w_l[layer, 1, 1], dup[1, hid_t:], 1, 0)
        ).astype(bf16)

    def context_grads(layer, s):
        dup[s, 0:hs] = mm(w_t[layer, s, 0, 3 * hs : 4 * hs], tmpb[0:tw], 1, 0).astype(bf16)
        dup[s, hs : hs + ls] = mm(w_l[layer, s, 0, 3 * ls : 4 * ls], tmpb[tw:width], 1, 0).astype(bf16)

    def attend_backward(layer, i):
        s, h = lax.div(i, heads), lax.rem(i, heads)
        queries = query(layer, s, h)
        key_text, key_lay = head_rows(layer, s, 1, h)
        keys = jnp.concatenate([key_text * HEAD**-0.5, key_lay * LHEAD**-0.5], axis=0).astype(bf16)
        values = jnp.concatenate(head_rows(layer, s, 2, h), axis=0)
        grads = jnp.concatenate([dup[s, at(h * HEAD, HEAD)], dup[s, at(hs + h * LHEAD, LHEAD)]], axis=0)
        low = probs[i]
        prob = low.astype(f32)
        dprob = mm(values, grads, 0, 0)
        inner = jnp.sum(dprob * prob, axis=0, keepdims=True)
        dscore = (prob * (dprob - inner)).astype(bf16)
        results = (mm(keys, dscore, 1, 0), mm(queries, dscore, 1, 1), mm(grads, low, 1, 1))
        for part, result in enumerate(results):
            result = result.astype(bf16)
            dqkv[s, at(part * hs + h * HEAD, HEAD)] = result[0:HEAD]
            dqkv[s, at(3 * hs + part * ls + h * LHEAD, LHEAD)] = result[HEAD:]

    def attend_grads(layer, s):
        text = jnp.concatenate(
            [mm(x_fm[layer, 0:tw], dqkv[s, 0 : 3 * hs], 1, 1), mm(tmpb[0:tw], ctx_t[layer, s], 1, 1)], axis=1
        )
        lay = jnp.concatenate(
            [mm(x_fm[layer, tw:width], dqkv[s, 3 * hs :], 1, 1), mm(tmpb[tw:width], ctx_l[layer, s], 1, 1)], axis=1
        )
        store_grad(layer, 0, s, text.astype(bf16), lay.astype(bf16))

    def attend_partial(layer):
        exs[0:tw] = (
            mm(w_t[layer, 0, 0, 0 : 3 * hs], dqkv[0, 0 : 3 * hs], 0, 0)
            + mm(w_t[layer, 1, 0, 0 : 3 * hs], dqkv[1, 0 : 3 * hs], 0, 0)
        ).astype(bf16)
        exs[tw:width] = (
            mm(w_l[layer, 0, 0, 0 : 3 * ls], dqkv[0, 3 * hs :], 0, 0)
            + mm(w_l[layer, 1, 0, 0 : 3 * ls], dqkv[1, 3 * hs :], 0, 0)
        ).astype(bf16)

    def small_sums(layer, s, row, ref, size):
        smsg[layer, s, row : row + 1, 0:size] = mm(ones, ref[s], 1, 1)[0:1]

    def first_grad(n, first, size, lanes):
        return acc[pl.ds(first, size), lanes] + exchanged(n, first, size, lanes)

    for layer in (1, 0):
        last = layer == 0
        n = 4 + 2 * (1 - layer)
        if last:
            load_columns(0)
            transit_load(1, 1)
        norm_backward(layer, 1, xh2, lambda s, z, lanes: g_fm[pl.ds(s, z), lanes].astype(f32))
        if last:
            transit_add(1, 1)
        for s in range(2):
            shrink_grads(layer, s)
        if last:
            transit_send(1, 1)
        ffn_backward(layer)
        grads_go(layer, 2)
        for s in range(2):
            expand_grads(layer, s)
        expand_partial(layer)
        swap = exchange_copy(n)
        swap.start()
        for s in range(2):
            small_sums(layer, s, 0, dup, hid_t + hid_l)
        grads_go(layer, 1)
        if last:
            transit_load(1, 0)
        swap.wait()
        norm_backward(layer, 0, xh1, functools.partial(first_grad, n))
        if last:
            transit_add(1, 0)
            p_load.wait()
        for s in range(2):
            context_grads(layer, s)
        if last:
            transit_send(1, 0)
        head = functools.partial(attend_backward, layer)
        loop(0, 3, head)
        transit_load(layer, 2)
        loop(3, 5, head)
        transit_add(layer, 2)
        loop(5, 6, head)
        if not last:
            p_load.start()
        for s in range(2):
            attend_grads(layer, s)
        transit_send(layer, 2)
        attend_partial(layer)
        swap = exchange_copy(n + 1)
        swap.start()
        for s in range(2):
            small_sums(layer, s, 1, dqkv, 3 * hs + 3 * ls)
        small_go(layer)
        grads_go(layer, 0)
        swap.wait()

        def finish(b):
            lanes = lanes_at(b * LANES, LANES)
            for first, size in streams:
                g_fm[pl.ds(first, size), lanes] = first_grad(n + 1, first, size, lanes).astype(bf16)

        loop(0, blocks, finish)
        finish_rows(layer, 0, out_pair)
        send_rows(layer, 2, back_pair, g_fm)

    transit(0, 1)
    small_total(1)
    final(1, 2, None)
    final(0, 2, None)
    transit(0, 0)
    small_total(0)
    final(1, 1, 2)
    final(0, 1, 2)
    final(1, 0, 1)
    final(0, 0, 1)

    for copy in small_z():
        copy.wait()
    if z_inside:
        for r in range(1, dp):
            ssum[...] = ssum[...] + szr[r - 1]
    sm_copy = local_copy(ssum, sm_out, so_sem.at[0])
    sm_copy.start()
    for layer in range(2):
        finish_rows(layer, 2, back_pair)

        @pl.when(c == layer)
        def _():
            for p in all_pieces:
                own_first(p).wait_send()
            if layer == 1:
                for p in all_pieces:
                    own_core(p).wait_send()

        @pl.when(c == zp)
        def _():
            for p in all_pieces:
                for copy in forwards(layer, p):
                    copy.wait_send()

        smalls = small_sends(layer)
        firsts = [first_sends(layer, chunk) for chunk in range(3)]
        for core in range(2):

            @pl.when(c == core)
            def _():
                for copy in smalls[core]:
                    copy.wait_send()
                for pair in firsts:
                    for copy in pair[core]:
                        copy.wait_send()

        for chunk in range(3):
            for copy in second_sends(layer, chunk):
                copy.wait_send()
    for r in order:
        sent(part_sends(0, r), z_inside and r > 0)
    if z_inside:
        for chunk in range(3):
            for r in range(1, dp):
                for copy in part_sends(chunk, r):
                    copy.wait_recv()
    sm_copy.wait()


def finishing(
    zr_t, zr_l, sums, rows_in_0, rows_in_1, rows_in_2, rows_in_3,
    rows_0, rows_1, rows_2, rows_3, att_t, out_t, exp_t, shr_t, att_l, out_l, exp_l, shr_l,
    bias_t, off_t, vec_t, bias_l, off_l, vec_l, sems,
):
    pairs = ((rows_in_0, rows_0), (rows_in_1, rows_1), (rows_in_2, rows_2), (rows_in_3, rows_3))
    copies = [pltpu.make_async_copy(src, dst, sems.at[i]) for i, (src, dst) in enumerate(pairs)]
    for copy in copies:
        copy.start()
    for zr, att, out, exp, shr in ((zr_t, att_t, out_t, exp_t, shr_t), (zr_l, att_l, out_l, exp_l, shr_l)):
        totals = []
        for chunk in range(3):
            total = zr[chunk, 0].astype(f32)
            for r in range(1, zr.shape[1]):
                total = total + zr[chunk, r].astype(f32)
            totals.append(total)
        size = out.shape[1]
        for j in range(3):
            att[j] = totals[0][:, j * size : (j + 1) * size]
        out[...] = totals[0][:, 3 * size : 4 * size]
        exp[...] = totals[1]
        shr[...] = totals[2]
    hs, ls = bias_t.shape[1], bias_l.shape[1]
    ft, fl = off_t.shape[1], off_l.shape[1]
    tw, lw = vec_t.shape[2], vec_l.shape[2]
    off_t[...] = sums[0:1, 0:ft]
    off_l[...] = sums[0:1, ft : ft + fl]
    bias_t[0:1] = sums[1:2, 0:hs]
    bias_t[1:2] = sums[1:2, 2 * hs : 3 * hs]
    bias_l[0:1] = sums[1:2, 3 * hs : 3 * hs + ls]
    bias_l[1:2] = sums[1:2, 3 * hs + 2 * ls : 3 * hs + 3 * ls]
    for row in range(6):
        vec_t[row] = sums[8 + row : 9 + row, 0:tw]
        vec_l[row] = sums[8 + row : 9 + row, tw : tw + lw]
    for copy in copies:
        copy.wait()


def local(
    dp,
    text_in,
    layout_in,
    text_cot,
    layout_cot,
    lengths,
    text_attend,
    text_biases,
    text_output,
    text_expand,
    text_offset,
    text_shrink,
    text_vectors,
    layout_attend,
    layout_biases,
    layout_output,
    layout_expand,
    layout_offset,
    layout_shrink,
    layout_vectors,
):
    rows, tw = text_in.shape[1:]
    lw = layout_in.shape[2]
    width, tokens = tw + lw, 2 * rows
    hs, ls = text_output.shape[2], layout_output.shape[2]
    ft, fl = text_expand.shape[2], layout_expand.shape[2]
    zt, zl = tw // dp, lw // dp
    z_inside = dp <= 4 and zt % 16 == 0 and zl % 16 == 0

    def shape(dims, dtype=bf16):
        return jax.ShapeDtypeStruct(dims, dtype)

    def attend_rows(attend):
        return attend[0].transpose(1, 2, 0).reshape(-1, attend.shape[1])

    hbm = pl.BlockSpec(memory_space=pltpu.HBM)
    vmem = pl.BlockSpec(memory_space=pltpu.VMEM)
    heads = hs // HEAD
    row_shapes = [shape((2, rows, tw)), shape((2, lw, rows)), shape((2, rows, tw)), shape((2, lw, rows))]
    out_shape = row_shapes + [
        shape((16, SMALL), f32),
        shape((3, tw, tw)), shape((3, lw, lw)),
        shape((3, dp, zt, tw)), shape((3, dp, zl, lw)),
        shape((2, 3, 2, tw, tw)), shape((2, 3, 2, lw, lw)),
        shape((2, 3, tw // 2, tw)), shape((2, 3, lw // 2, lw)),
        shape((3, 2, tw, tw)), shape((3, 2, lw, lw)),
        shape((3, tw, tw)), shape((3, lw, lw)),
        shape((2 * heads, tokens, tokens)),
    ]
    dma = pltpu.SemaphoreType.DMA
    scratch = [
        pltpu.VMEM((2, 2, 3, tw, tw), bf16),
        pltpu.VMEM((2, 2, 3, lw, lw), bf16),
        pltpu.VMEM((2, 2, 16, SMALL), bf16),
        pltpu.VMEM((2, 16, SMALL), f32),
        pltpu.VMEM((16, SMALL), bf16),
        pltpu.VMEM((16, SMALL), f32),
        pltpu.VMEM((tokens, LANES), f32),
        pltpu.VMEM((tokens, tw), bf16),
        pltpu.VMEM((lw, tokens), bf16),
        pltpu.VMEM((2, width, tokens), bf16),
        pltpu.VMEM((2, 2, 3 * hs, tokens), bf16),
        pltpu.VMEM((2, 2, 3 * ls, tokens), bf16),
        pltpu.VMEM((2 * heads, tokens, tokens), bf16),
        pltpu.VMEM((2, 2, hs, tokens), bf16),
        pltpu.VMEM((2, 2, ls, tokens), bf16),
        pltpu.VMEM((2, width, tokens), bf16),
        pltpu.VMEM((2, width, tokens), bf16),
        pltpu.VMEM((2, width, tokens), bf16),
        pltpu.VMEM((2, 2, ft + fl, tokens), bf16),
        pltpu.VMEM((2, 2, ft + fl, tokens), bf16),
        pltpu.VMEM((2, 8, tokens), f32),
        pltpu.VMEM((width, tokens), f32),
        pltpu.VMEM((width, tokens), bf16),
        pltpu.VMEM((2, width, tokens), bf16),
        pltpu.VMEM((width, tokens), bf16),
        pltpu.VMEM((width, tokens), bf16),
        pltpu.VMEM((2, ft + fl, tokens), bf16),
        pltpu.VMEM((2, 3 * hs + 3 * ls, tokens), bf16),
        pltpu.VMEM((3, SMALL, 16), f32),
        pltpu.VMEM((2, tw, tw), bf16),
        pltpu.VMEM((2, lw, lw), bf16),
        pltpu.VMEM((2, tw // 2, tw), bf16),
        pltpu.VMEM((2, lw // 2, lw), bf16),
        pltpu.VMEM((3, tw, tw), bf16),
        pltpu.VMEM((3, lw, lw), bf16),
        pltpu.VMEM((2, 2, 16, SMALL), f32),
        pltpu.VMEM((4, 16, SMALL), f32),
        pltpu.VMEM((16, SMALL), f32),
        pltpu.VMEM((3, 16, SMALL), f32),
        dma((2, 2, 17)), dma((17, 2)), dma((2, 17, 2)), dma((3,)), dma((4, 5)), dma((8,)), dma((8,)),
        dma((4, 3)), dma((2, 2)), dma((2,)),
        dma((2, 3, 2, 3)), dma((2, 3, 2)), dma((2, 3, 2)), dma((3, 2, 2, 2)), dma((3, 2)), dma((3, 2)),
        dma((3, 2, 4)), dma((3, 2, 4)), dma((2, 3)), dma((2, 3, 4)), dma((2, 4)),
        dma((2, 2)), dma((4,)), dma((3,)), dma((3,)), dma((1,)),
    ]
    results = pl.pallas_call(
        functools.partial(kernel, dp, z_inside),
        out_shape=out_shape,
        in_specs=[hbm] * 12 + [vmem] * 6 + [pl.BlockSpec(memory_space=pltpu.SMEM)],
        out_specs=[hbm] * len(out_shape),
        scratch_shapes=scratch,
        compiler_params=pltpu.CompilerParams(
            collective_id=0, has_side_effects=True, vmem_limit_bytes=63 * 1024 * 1024
        ),
    )(
        text_in, layout_in.transpose(0, 2, 1), text_cot, layout_cot.transpose(0, 2, 1),
        attend_rows(text_attend), text_output[0].T, text_expand[0], text_shrink[0],
        attend_rows(layout_attend), layout_output[0].T, layout_expand[0], layout_shrink[0],
        text_biases[0], layout_biases[0], text_offset, layout_offset, text_vectors[0], layout_vectors[0], lengths,
    )
    row_results, sums = results[:4], results[4]
    if z_inside:
        parts_t, parts_l = results[7], results[8]
    else:
        parts_t = lax.psum_scatter(results[5], "dp", scatter_dimension=1, tiled=True)[:, None]
        parts_l = lax.psum_scatter(results[6], "dp", scatter_dimension=1, tiled=True)[:, None]
        sums = lax.psum(sums, "dp")
    final_shapes = row_shapes + [
        shape((3, zt, hs), f32), shape((zt, hs), f32), shape((zt, ft), f32), shape((zt, ft), f32),
        shape((3, zl, ls), f32), shape((zl, ls), f32), shape((zl, fl), f32), shape((zl, fl), f32),
        shape((2, hs), f32), shape((1, ft), f32), shape((6, 1, tw), f32),
        shape((2, ls), f32), shape((1, fl), f32), shape((6, 1, lw), f32),
    ]
    (
        text_out, lay_out, text_back, lay_back, att_t, out_t, exp_t, shr_t, att_l, out_l, exp_l, shr_l,
        bias_t, off_t, vec_t, bias_l, off_l, vec_l,
    ) = pl.pallas_call(
        finishing,
        out_shape=final_shapes,
        in_specs=[vmem] * 3 + [hbm] * 4,
        out_specs=[hbm] * 4 + [vmem] * 14,
        scratch_shapes=[dma((4,))],
        compiler_params=pltpu.CompilerParams(vmem_limit_bytes=32 * 1024 * 1024),
    )(parts_t, parts_l, sums, *row_results)
    return (
        text_out[None],
        lay_out.transpose(0, 2, 1)[None],
        text_back[None],
        lay_back.transpose(0, 2, 1)[None],
        att_t.transpose(1, 0, 2)[None],
        bias_t[None],
        out_t[None],
        exp_t[None],
        off_t,
        shr_t[None],
        vec_t.transpose(1, 0, 2),
        att_l.transpose(1, 0, 2)[None],
        bias_l[None],
        out_l[None],
        exp_l[None],
        off_l,
        shr_l[None],
        vec_l.transpose(1, 0, 2),
    )


def solution(mesh):
    return jax.shard_map(
        functools.partial(local, mesh.shape["dp"]),
        mesh=mesh,
        in_specs=(
            P(None, ("dp", "tensor"), None),
            P(None, ("dp", "tensor"), None),
            P(None, ("dp", "tensor"), None),
            P(None, ("dp", "tensor"), None),
            P(None, "dp"),
            P("section", None, None, "tensor"),
            P("section", None, "tensor"),
            P("section", None, "tensor"),
            P("section", None, "tensor"),
            P("section", "tensor"),
            P("section", None, "tensor"),
            P("section", None, None),
            P("section", None, None, "tensor"),
            P("section", None, "tensor"),
            P("section", None, "tensor"),
            P("section", None, "tensor"),
            P("section", "tensor"),
            P("section", None, "tensor"),
            P("section", None, None),
        ),
        out_specs=(
            P("section", None, ("dp", "tensor"), None),
            P("section", None, ("dp", "tensor"), None),
            P("section", None, ("dp", "tensor"), None),
            P("section", None, ("dp", "tensor"), None),
            P("section", "dp", None, "tensor"),
            P("section", None, "tensor"),
            P("section", "dp", "tensor"),
            P("section", "dp", "tensor"),
            P("section", "tensor"),
            P("section", "dp", "tensor"),
            P("section", None, None),
            P("section", "dp", None, "tensor"),
            P("section", None, "tensor"),
            P("section", "dp", "tensor"),
            P("section", "dp", "tensor"),
            P("section", "tensor"),
            P("section", "dp", "tensor"),
            P("section", None, None),
        ),
        check_vma=False,
    )
```

profile of v0, /device:TPU:0, one launch (start us, length us, event | category | flops | bytes accessed | tf_op | source)
XLA Modules:
  0.0 319.9 jit_solution(2852292207879208767)
XLA Ops:
  0.7 308.4 %shard_map.322 = (bf16[2,256,768]{2,1,0:T(8,128)(2,1)}, bf16[2,192,256]{2,1,0:T(8,128)(2,1)}, bf16[2,256,768]{2,1,0:T(8,128)(2,1)}, bf16[2,192,256]{2,1,0:T(8,12...) custom-call(bf16[2,256,768]{2,1,0:T(8,128)(2,1)} %text_in.1, ...), custom_call_target="tpu_custom_call" | custom-call | tf_op jit(solution)/shard_map/pallas_call | solution.py:1061
  309.0 0.0 copy-start
  309.1 2.0 copy-done
  311.0 0.0 copy-start.1
  311.0 1.1 copy-done.1
  312.2 0.0 copy-start.2
  312.2 1.1 copy-done.2
  313.3 0.0 copy-start.3
  313.3 1.0 copy-done.3
  314.3 0.0 copy-start.4
  314.3 0.9 copy-done.4
  315.2 0.0 copy-start.5
  315.2 0.9 copy-done.5
  316.1 0.0 copy-start.6
  316.1 0.8 copy-done.6
  317.0 2.7 shard_map.323
Async XLA Ops:
  309.0 2.0 copy-start
  311.0 1.1 copy-start.1
  312.2 1.1 copy-start.2
  313.3 1.0 copy-start.3
  314.3 0.9 copy-start.4
  315.2 0.9 copy-start.5
  316.1 0.8 copy-start.6
where the time goes:
time: 326 us; the launch traced here: 320 us
  Pallas kernels  311 us (95%)
  local copies, waits for them, and re-layouts  7.91 us (2%)
    pallas_call x1, Pallas kernels, local(): pl.pallas_call(functools.partial(kernel, dp, z_inside), out_shape=out_sha...  308 us
    unnamed x14, local copies, waits for them, and re-layouts  7.91 us

commit v1 on v0

--- a/solution.py
+++ b/solution.py
@@ -48,12 +48,13 @@
     text_in, lay_in, text_cot, lay_cot, att_t, out_t, exp_t, shr_t, att_l, out_l, exp_l, shr_l,
     bias_t, bias_l, off_t, off_l, vec_t, vec_l, lengths,
     text_out, lay_out, text_back, lay_back, sm_out,
-    zs_t, zs_l, zr_t, zr_l, gb_t, gb_l, r1_t, r1_l, r2_t, r2_l, ro_t, ro_l, p_keep,
+    zs_t, zs_l, zr_t, zr_l, gb_t, gb_l, rz_t, rz_l, r1_t, r1_l, r2_t, r2_l, ro_t, ro_l, p_keep,
     w_t, w_l, small, vecs, own_small, own_vec, key_bias, rows_t, rows_l, x_fm, qkv_t, qkv_l, probs,
     ctx_t, ctx_l, xh1, n1b, xh2, act, gp, stats, acc, exs, exr, tmpb, g_fm, dup, dqkv, cols,
-    stg_t, stg_l, tv_t, tv_l, fv_t, fv_l, smsg, srec, ssum, szr,
+    stg_t, stg_l, zv_t, zv_l, tv_t, tv_l, fv_t, fv_l, smsg, srec, ssum, szr,
     ag_recv, ag_own, ag_fwd, vec_sem, row_sem, ex_send, ex_recv, out_sem, stg_sem, p_sem,
-    s1_send, s1_recv, s2_send, s2_recv, so_send, so_recv, z_send, z_recv, tv_sem, fv_sem, zo_sem,
+    rz_send, rz_recv, s1_send, d_send, r1_recv, s2_send, s2_recv, so_send, so_recv, z_send, z_recv,
+    zv_sem, tv_sem, fv_sem,
     sm_send, sm_recv, sz_send, sz_recv, so_sem,
 ):
     c = lax.axis_index("section")
@@ -76,7 +77,7 @@
     hs, ls = out_t.shape[0], out_l.shape[0]
     heads = hs // HEAD
     blocks = tokens // LANES
-    th, lh = tw // 2, lw // 2
+    tq, lq = tw // 4, lw // 4
     streams = ((0, tw), (tw, lw))
     z_peers = [lax.rem(d + r, dp) for r in range(1, dp)] if z_inside else [dz]
 
@@ -380,11 +381,17 @@
             )
         return copies
 
-    def send_rows(layer, base, dest_pair, value):
+    def stage_rows(layer, value):
         @pl.when(c == layer)
         def _():
             rows_t[...] = value[0:tw].T
             rows_l[...] = value[tw:width]
+
+    def send_rows(layer, base, dest_pair, value):
+        stage_rows(layer, value)
+
+        @pl.when(c == layer)
+        def _():
             start(rows_out(base, *dest_pair))
 
     def finish_rows(layer, base, dest_pair):
@@ -462,10 +469,10 @@
         swap.wait()
         if not last:
             second_norm(0, 1, x_fm.at[1])
-            send_rows(0, 0, out_pair, x_fm.at[1])
             need(1, 0)
             load_columns(1)
         else:
+            send_rows(0, 0, out_pair, x_fm.at[1])
             second_norm(1, 3, tmpb)
             send_rows(1, 0, out_pair, tmpb)
 
@@ -480,87 +487,133 @@
         stg_l[s] = lay_value
         start(grad_store(layer, chunk, s))
 
+    groups = (
+        (gb_t, rz_t, r1_t, r2_t, ro_t, zs_t, zr_t, zv_t, tv_t, fv_t, w_t, tq),
+        (gb_l, rz_l, r1_l, r2_l, ro_l, zs_l, zr_l, zv_l, tv_l, fv_l, w_l, lq),
+    )
+    tx = t1 + c * (t2 - t1)
+    near, far = 2 * zp, 2 * (1 - zp)
+
+    def quarters(first, count, size):
+        return at(first * size, count * size)
+
     def first_sends(layer, chunk):
-        zero, one = [], []
-        for k, (grad, come, total, size) in enumerate(((gb_t, r1_t, r2_t, th), (gb_l, r1_l, r2_l, lh))):
-            h1, h2 = pl.ds(0, size), pl.ds(size, size)
-            zero.append(
-                remote(
-                    grad.at[layer, chunk, 1, h1], total.at[chunk, 0, h1],
-                    s1_send.at[layer, chunk, k, 0], s2_recv.at[chunk, 0, 0, k], (layer, d, t1),
-                )
-            )
-            one.append(
-                remote(
-                    grad.at[layer, chunk, 1, h1], come.at[layer, chunk],
-                    s1_send.at[layer, chunk, k, 0], s1_recv.at[layer, chunk, k], (1, d, t1),
-                )
-            )
-            one.append(
-                remote(
-                    grad.at[layer, chunk, 1, h2], come.at[layer, chunk],
-                    s1_send.at[layer, chunk, k, 1], s1_recv.at[layer, chunk, k], (0, d, t2),
-                )
-            )
-            one.append(
-                remote(
-                    grad.at[layer, chunk, 0, h2], total.at[chunk, 1, h2],
-                    s1_send.at[layer, chunk, k, 2], s2_recv.at[chunk, 1, 1, k], (layer, d, t2),
-                )
-            )
-        if layer == 1:
-            for k, (grad, arrive) in enumerate(((gb_t, ro_t), (gb_l, ro_l))):
-                zero.append(
+        copies = []
+        for g, (gb, rz, r1, r2, ro, zs, zr, zv, tv, fv, w, size) in enumerate(groups):
+            for i, rows in enumerate((quarters(far, 2, size), quarters(near + c, 1, size))):
+                copies.append(
                     remote(
-                        grad.at[1, chunk, 0], arrive.at[chunk], so_send.at[chunk, k], so_recv.at[chunk, k], other
+                        gb.at[layer, chunk, 1 - c, rows], r2.at[chunk, c, rows],
+                        s1_send.at[layer, chunk, g, i], s2_recv.at[chunk, c, i, g], (layer, d, tx),
                     )
                 )
-        return zero, one
+        return copies
+
+    def own_sends(chunk):
+        return [
+            remote(gb.at[1, chunk, 0], ro.at[chunk], so_send.at[chunk, g], so_recv.at[chunk, g], other)
+            for g, (gb, rz, r1, r2, ro, *_) in enumerate(groups)
+        ]
+
+    def pair_sends(layer, chunk):
+        return [
+            remote(
+                gb.at[layer, chunk, 1, quarters(far, 2, size)], rz.at[layer, chunk],
+                rz_send.at[layer, chunk, g], rz_recv.at[layer, chunk, g], (1, dz, t),
+            )
+            for g, (gb, rz, *_, size) in enumerate(groups)
+        ]
 
     def grads_go(layer, chunk):
         for s in range(2):
             wait(grad_store(layer, chunk, s))
-        zero, one = first_sends(layer, chunk)
-
-        @pl.when(c == 0)
-        def _():
-            start(zero)
 
         @pl.when(c == 1)
         def _():
-            start(one)
-
-    tx = t1 + c * (t2 - t1)
-    transit_groups = ((gb_t, r1_t, r2_t, th, tv_t), (gb_l, r1_l, r2_l, lh, tv_l))
-
-    def mine(grad, layer, chunk, size):
-        return grad.at[layer, chunk, 1 - c, at((1 - c) * size, size)]
+            start(pair_sends(layer, chunk))
+
+        if layer == 1:
+
+            @pl.when(c == 0)
+            def _():
+                start(own_sends(chunk))
+
+        start(first_sends(layer, chunk))
+
+    def pair_loads(layer, chunk):
+        copies = []
+        for g, (gb, rz, r1, r2, ro, zs, zr, zv, tv, fv, w, size) in enumerate(groups):
+            copies.append(local_copy(gb.at[layer, chunk, 1, quarters(near, 2, size)], zv.at[0], zv_sem.at[g, 0]))
+            copies.append(local_copy(rz.at[layer, chunk], zv.at[1], zv_sem.at[g, 1]))
+        return copies
+
+    def pair_stores(layer, chunk):
+        return [
+            local_copy(zv.at[0], gb.at[layer, chunk, 1, quarters(near, 2, size)], zv_sem.at[g, 2])
+            for g, (gb, rz, r1, r2, ro, zs, zr, zv, tv, fv, w, size) in enumerate(groups)
+        ]
+
+    def diagonal_sends(layer, chunk):
+        copies = []
+        for g, (gb, rz, r1, *_, size) in enumerate(groups):
+            for i, device in enumerate(((1, d, t1), (0, d, t2))):
+                copies.append(
+                    remote(
+                        gb.at[layer, chunk, 1, quarters(near + i, 1, size)], r1.at[layer, chunk],
+                        d_send.at[layer, chunk, g, i], r1_recv.at[layer, chunk, g], device,
+                    )
+                )
+        return copies
+
+    def pair_load(layer, chunk):
+        @pl.when(c == 1)
+        def _():
+            for g, (gb, rz, *_) in enumerate(groups):
+                landed(rz.at[layer, chunk], rz_recv.at[layer, chunk, g])
+            start(pair_loads(layer, chunk))
+
+    def pair_add(layer, chunk):
+        @pl.when(c == 1)
+        def _():
+            wait(pair_loads(layer, chunk))
+            for zv in (zv_t, zv_l):
+                zv[0] = (zv[0].astype(f32) + zv[1].astype(f32)).astype(bf16)
+            start(pair_stores(layer, chunk))
+
+    def pair_send(layer, chunk):
+        @pl.when(c == 1)
+        def _():
+            wait(pair_stores(layer, chunk))
+            start(diagonal_sends(layer, chunk))
+
+    def waiting(gb, layer, chunk, size):
+        return gb.at[layer, chunk, 1 - c, quarters(near + 1 - c, 1, size)]
+
+    def transit_loads(layer, chunk):
+        copies = []
+        for g, (gb, rz, r1, r2, ro, zs, zr, zv, tv, fv, w, size) in enumerate(groups):
+            copies.append(local_copy(waiting(gb, layer, chunk, size), tv.at[0], tv_sem.at[g, 0]))
+            copies.append(local_copy(r1.at[layer, chunk], tv.at[1], tv_sem.at[g, 1]))
+        return copies
+
+    def transit_stores(layer, chunk):
+        return [
+            local_copy(tv.at[0], waiting(gb, layer, chunk, size), tv_sem.at[g, 2])
+            for g, (gb, rz, r1, r2, ro, zs, zr, zv, tv, fv, w, size) in enumerate(groups)
+        ]
 
     def second_sends(layer, chunk):
         return [
             remote(
-                mine(grad, layer, chunk, size), total.at[chunk, c, at((1 - c) * size, size)],
-                s2_send.at[layer, chunk, k], s2_recv.at[chunk, c, 1 - c, k], (layer, d, tx),
+                waiting(gb, layer, chunk, size), r2.at[chunk, c, quarters(near + 1 - c, 1, size)],
+                s2_send.at[layer, chunk, g], s2_recv.at[chunk, c, 2, g], (layer, d, tx),
             )
-            for k, (grad, come, total, size, tv) in enumerate(transit_groups)
+            for g, (gb, rz, r1, r2, *_, size) in enumerate(groups)
         ]
 
-    def transit_loads(layer, chunk):
-        copies = []
-        for k, (grad, come, total, size, tv) in enumerate(transit_groups):
-            copies.append(local_copy(mine(grad, layer, chunk, size), tv.at[0], tv_sem.at[k, 0]))
-            copies.append(local_copy(come.at[layer, chunk], tv.at[1], tv_sem.at[k, 1]))
-        return copies
-
-    def transit_stores(layer, chunk):
-        return [
-            local_copy(tv.at[0], mine(grad, layer, chunk, size), tv_sem.at[k, 2])
-            for k, (grad, come, total, size, tv) in enumerate(transit_groups)
-        ]
-
     def transit_load(layer, chunk):
-        for k, (grad, come, total, size, tv) in enumerate(transit_groups):
-            landed(come.at[layer, chunk], s1_recv.at[layer, chunk, k])
+        for g, (gb, rz, r1, *_) in enumerate(groups):
+            landed(r1.at[layer, chunk], r1_recv.at[layer, chunk, g])
         start(transit_loads(layer, chunk))
 
     def transit_add(layer, chunk):
@@ -573,77 +626,94 @@
         wait(transit_stores(layer, chunk))
         start(second_sends(layer, chunk))
 
-    def transit(layer, chunk):
-        transit_load(layer, chunk)
-        transit_add(layer, chunk)
-        transit_send(layer, chunk)
-
-    parts = dp if z_inside else 2
-    final_groups = ((gb_t, ro_t, r2_t, fv_t, zs_t, zr_t), (gb_l, ro_l, r2_l, fv_l, zs_l, zr_l))
-
-    def part_sends(chunk, r):
+    def final_loads(layer, chunk, stage):
+        first = near if stage else far
         copies = []
-        for k, (grad, arrive, total, fv, zs, zr) in enumerate(final_groups):
-            size = fv.shape[1] // parts
+        for g, (gb, rz, r1, r2, ro, zs, zr, zv, tv, fv, w, size) in enumerate(groups):
+            rows = quarters(first, 2, size)
+            own = ro.at[chunk, rows] if layer == 1 else gb.at[0, chunk, 0, rows]
+            places = (w.at[1, 0, chunk, rows], w.at[1, 1, chunk, rows], fv.at[chunk, rows])
+            for i, src in enumerate((own, r2.at[chunk, 0, rows], r2.at[chunk, 1, rows])):
+                copies.append(local_copy(src, places[i], fv_sem.at[chunk, stage, g, i]))
+        return copies
+
+    def final_load(layer, chunk, stage):
+        @pl.when(c == layer)
+        def _():
+            for g, (gb, rz, r1, r2, ro, zs, zr, zv, tv, fv, w, size) in enumerate(groups):
+                for way in range(2):
+                    if stage == 0:
+                        landed(r2.at[chunk, way, quarters(far, 2, size)], s2_recv.at[chunk, way, 0, g])
+                    else:
+                        landed(r2.at[chunk, way, quarters(near + way, 1, size)], s2_recv.at[chunk, way, 1, g])
+                        landed(r2.at[chunk, way, quarters(near + 1 - way, 1, size)], s2_recv.at[chunk, way, 2, g])
+                if layer == 1 and stage == 0:
+                    landed(ro.at[chunk], so_recv.at[chunk, g])
+            start(final_loads(layer, chunk, stage))
+
+    def z_send_of(chunk, stage, i, g):
+        gb, rz, r1, r2, ro, zs, zr, zv, tv, fv, w, size = groups[g]
+        j = (near if stage else far) + i
+        return j, w.at[1, 0, chunk, quarters(j, 1, size)], zr.at[chunk, d]
+
+    def z_remote(chunk, stage, i, g):
+        j, piece, dest = z_send_of(chunk, stage, i, g)
+        return remote(piece, dest, z_send.at[chunk, stage, i, g], z_recv.at[chunk, d, g], (c, j, t))
+
+    def sum_stores(chunk, stage):
+        first = near if stage else far
+        return [
+            local_copy(
+                w.at[1, 0, chunk, quarters(first, 2, size)], zs.at[chunk, quarters(first, 2, size)],
+                z_send.at[chunk, stage, 0, g],
+            )
+            for g, (gb, rz, r1, r2, ro, zs, zr, zv, tv, fv, w, size) in enumerate(groups)
+        ]
+
+    def final_add(layer, chunk, stage):
+        @pl.when(c == layer)
+        def _():
+            wait(final_loads(layer, chunk, stage))
+            for gb, rz, r1, r2, ro, zs, zr, zv, tv, fv, w, size in groups:
+                rows = quarters(near if stage else far, 2, size)
+                total = w[1, 0, chunk, rows].astype(f32) + w[1, 1, chunk, rows].astype(f32)
+                w[1, 0, chunk, rows] = (total + fv[chunk, rows].astype(f32)).astype(bf16)
             if not z_inside:
-                rows = pl.ds(r * size, size)
-                copies.append(local_copy(fv.at[0, rows], zs.at[chunk, rows], zo_sem.at[k, r]))
-                continue
-            j = lax.rem(d + r, dp)
-            piece = fv.at[0, at(j * size, size)]
-            if r == 0:
-                copies.append(local_copy(piece, zr.at[chunk, 0], zo_sem.at[k, 0]))
-            else:
-                copies.append(
-                    remote(piece, zr.at[chunk, r], z_send.at[chunk, k, r], z_recv.at[chunk, k, r], (c, j, t))
-                )
-        return copies
-
-    def part_rows(r, size):
-        if not z_inside:
-            return pl.ds(r * size, size)
-        return at(lax.rem(d + r, dp) * size, size)
-
-    def part_loads(layer, chunk, r):
-        copies = []
-        for k, (grad, arrive, total, fv, zs, zr) in enumerate(final_groups):
-            rows = part_rows(r, fv.shape[1] // parts)
-            own = arrive.at[chunk, rows] if layer == 1 else grad.at[layer, chunk, 0, rows]
-            for i, src in enumerate((own, total.at[chunk, 0, rows], total.at[chunk, 1, rows])):
-                copies.append(local_copy(src, fv.at[i, rows], fv_sem.at[k, i, r]))
-        return copies
-
-    order = list(range(1, parts)) + [0]
-
-    def sent(copies, inside):
-        for copy in copies:
-            if inside:
-                copy.wait_send()
-            else:
-                copy.wait()
-
-    def final(layer, chunk, before):
-        @pl.when(c == layer)
-        def _():
-            if before is not None:
-                for r in order:
-                    sent(part_sends(before, r), z_inside and r > 0)
-            for k, (grad, arrive, total, fv, zs, zr) in enumerate(final_groups):
-                size = (th, lh)[k]
-                for way in range(2):
-                    for h in range(2):
-                        landed(total.at[chunk, way, pl.ds(h * size, size)], s2_recv.at[chunk, way, h, k])
-                if layer == 1:
-                    landed(arrive.at[chunk], so_recv.at[chunk, k])
-            for r in order:
-                start(part_loads(layer, chunk, r))
-            for r in order:
-                wait(part_loads(layer, chunk, r))
-                for grad, arrive, total, fv, zs, zr in final_groups:
-                    rows = part_rows(r, fv.shape[1] // parts)
-                    summed = fv[0, rows].astype(f32) + fv[1, rows].astype(f32) + fv[2, rows].astype(f32)
-                    fv[0, rows] = summed.astype(bf16)
-                start(part_sends(chunk, r))
+                start(sum_stores(chunk, stage))
+                return
+            for i in range(2):
+                for g in range(2):
+                    j, piece, dest = z_send_of(chunk, stage, i, g)
+
+                    @pl.when(j != d)
+                    def _():
+                        z_remote(chunk, stage, i, g).start()
+
+                    @pl.when(j == d)
+                    def _():
+                        local_copy(piece, dest, z_recv.at[chunk, d, g]).start()
+
+    def final(layer, chunk, stage):
+        final_load(layer, chunk, stage)
+        final_add(layer, chunk, stage)
+
+    def sums_done():
+        for chunk in range(3):
+            for stage in range(2):
+                if not z_inside:
+                    wait(sum_stores(chunk, stage))
+                    continue
+                for i in range(2):
+                    for g in range(2):
+
+                        @pl.when(z_send_of(chunk, stage, i, g)[0] != d)
+                        def _():
+                            z_remote(chunk, stage, i, g).wait_send()
+
+            if z_inside:
+                for j in range(dp):
+                    for g in range(2):
+                        landed(groups[g][6].at[chunk, j], z_recv.at[chunk, j, g])
 
     def small_sends(layer):
         zero = [remote(smsg.at[layer, 1], srec.at[0], sm_send.at[layer, 0], sm_recv.at[0], (layer, d, t1))]
@@ -800,51 +870,97 @@
     def first_grad(n, first, size, lanes):
         return acc[pl.ds(first, size), lanes] + exchanged(n, first, size, lanes)
 
+    def gather_sent():
+        for layer in range(2):
+
+            @pl.when(c == layer)
+            def _():
+                for p in all_pieces:
+                    own_first(p).wait_send()
+                    if layer == 1:
+                        own_core(p).wait_send()
+
+            @pl.when(c == zp)
+            def _():
+                for p in all_pieces:
+                    for copy in forwards(layer, p):
+                        copy.wait_send()
+
+    def run(*tasks):
+        for task in tasks:
+            task[0](*task[1:])
+
+    Z, T, F = (pair_load, pair_add, pair_send), (transit_load, transit_add, transit_send), (final_load, final_add)
+    service = {
+        (1, "context"): [(Z[0], 1, 2)],
+        (1, "heads 0"): [(Z[1], 1, 2)],
+        (1, "heads 1"): [(Z[2], 1, 2), (Z[0], 1, 1)],
+        (1, "heads 2"): [(Z[1], 1, 1)],
+        (1, "attend grads"): [(Z[2], 1, 1)],
+        (1, "swap"): [(T[0], 1, 2)],
+        (1, "swapped"): [(T[1], 1, 2)],
+        (1, "finished"): [(T[2], 1, 2)],
+        (0, "begin"): [(gather_sent,), (T[0], 1, 1)],
+        (0, "second norm"): [(T[1], 1, 1), (Z[0], 1, 0), (F[0], 1, 2, 0)],
+        (0, "shrink grads"): [(T[2], 1, 1), (Z[1], 1, 0)],
+        (0, "ffn"): [(Z[2], 1, 0), (F[1], 1, 2, 0)],
+        (0, "expand grads"): [(T[0], 1, 0), (F[0], 1, 2, 1)],
+        (0, "ffn swap"): [(F[1], 1, 2, 1)],
+        (0, "first norm"): [(T[1], 1, 0), (F[0], 1, 1, 0), (Z[0], 0, 2)],
+        (0, "context"): [(T[2], 1, 0)],
+        (0, "heads 0"): [(Z[1], 0, 2), (F[1], 1, 1, 0), (F[0], 1, 1, 1)],
+        (0, "heads 1"): [(Z[2], 0, 2), (Z[0], 0, 1), (F[1], 1, 1, 1)],
+        (0, "heads 2"): [(Z[1], 0, 1), (T[0], 0, 2), (F[0], 1, 0, 0)],
+        (0, "attend grads"): [(Z[2], 0, 1), (T[1], 0, 2), (F[1], 1, 0, 0)],
+        (0, "swap"): [(T[2], 0, 2), (F[0], 1, 0, 1)],
+        (0, "finished"): [(F[1], 1, 0, 1)],
+    }
+
     for layer in (1, 0):
         last = layer == 0
         n = 4 + 2 * (1 - layer)
+
+        def point(name):
+            run(*service.get((layer, name), []))
+
         if last:
             load_columns(0)
-            transit_load(1, 1)
+        point("begin")
         norm_backward(layer, 1, xh2, lambda s, z, lanes: g_fm[pl.ds(s, z), lanes].astype(f32))
-        if last:
-            transit_add(1, 1)
+        point("second norm")
         for s in range(2):
             shrink_grads(layer, s)
-        if last:
-            transit_send(1, 1)
+        point("shrink grads")
         ffn_backward(layer)
         grads_go(layer, 2)
+        point("ffn")
         for s in range(2):
             expand_grads(layer, s)
+        point("expand grads")
         expand_partial(layer)
         swap = exchange_copy(n)
         swap.start()
         for s in range(2):
             small_sums(layer, s, 0, dup, hid_t + hid_l)
         grads_go(layer, 1)
-        if last:
-            transit_load(1, 0)
+        point("ffn swap")
         swap.wait()
         norm_backward(layer, 0, xh1, functools.partial(first_grad, n))
+        point("first norm")
         if last:
-            transit_add(1, 0)
             p_load.wait()
         for s in range(2):
             context_grads(layer, s)
-        if last:
-            transit_send(1, 0)
+        point("context")
         head = functools.partial(attend_backward, layer)
-        loop(0, 3, head)
-        transit_load(layer, 2)
-        loop(3, 5, head)
-        transit_add(layer, 2)
-        loop(5, 6, head)
+        for i in range(3):
+            loop(2 * i, 2 * i + 2, head)
+            point(f"heads {i}")
         if not last:
             p_load.start()
         for s in range(2):
             attend_grads(layer, s)
-        transit_send(layer, 2)
+        point("attend grads")
         attend_partial(layer)
         swap = exchange_copy(n + 1)
         swap.start()
@@ -852,7 +968,9 @@
             small_sums(layer, s, 1, dqkv, 3 * hs + 3 * ls)
         small_go(layer)
         grads_go(layer, 0)
+        point("swap")
         swap.wait()
+        point("swapped")
 
         def finish(b):
             lanes = lanes_at(b * LANES, LANES)
@@ -860,19 +978,17 @@
                 g_fm[pl.ds(first, size), lanes] = first_grad(n + 1, first, size, lanes).astype(bf16)
 
         loop(0, blocks, finish)
+        point("finished")
         finish_rows(layer, 0, out_pair)
-        send_rows(layer, 2, back_pair, g_fm)
-
-    transit(0, 1)
-    small_total(1)
-    final(1, 2, None)
-    final(0, 2, None)
-    transit(0, 0)
-    small_total(0)
-    final(1, 1, 2)
-    final(0, 1, 2)
-    final(1, 0, 1)
-    final(0, 0, 1)
+        stage_rows(layer, g_fm)
+
+    run(
+        *((step, 0, 1) for step in T), *((step, 0, 0) for step in Z),
+        (final, 0, 2, 0), (final, 0, 2, 1), (small_total, 1), (final, 0, 1, 0),
+        *((step, 0, 0) for step in T),
+    )
+    start(rows_out(2, *back_pair))
+    run((small_total, 0), (final, 0, 1, 1), (final, 0, 0, 0), (final, 0, 0, 1))
 
     for copy in small_z():
         copy.wait()
@@ -881,57 +997,48 @@
             ssum[...] = ssum[...] + szr[r - 1]
     sm_copy = local_copy(ssum, sm_out, so_sem.at[0])
     sm_copy.start()
+    wait(rows_out(2, *back_pair))
     for layer in range(2):
-        finish_rows(layer, 2, back_pair)
-
-        @pl.when(c == layer)
-        def _():
-            for p in all_pieces:
-                own_first(p).wait_send()
-            if layer == 1:
-                for p in all_pieces:
-                    own_core(p).wait_send()
-
-        @pl.when(c == zp)
-        def _():
-            for p in all_pieces:
-                for copy in forwards(layer, p):
-                    copy.wait_send()
-
         smalls = small_sends(layer)
-        firsts = [first_sends(layer, chunk) for chunk in range(3)]
         for core in range(2):
 
             @pl.when(c == core)
             def _():
                 for copy in smalls[core]:
                     copy.wait_send()
-                for pair in firsts:
-                    for copy in pair[core]:
-                        copy.wait_send()
+                for chunk in range(3):
+                    if core == 1:
+                        for copy in pair_sends(layer, chunk) + diagonal_sends(layer, chunk):
+                            copy.wait_send()
+                    elif layer == 1:
+                        for copy in own_sends(chunk):
+                            copy.wait_send()
 
         for chunk in range(3):
-            for copy in second_sends(layer, chunk):
+            for copy in first_sends(layer, chunk) + second_sends(layer, chunk):
                 copy.wait_send()
-    for r in order:
-        sent(part_sends(0, r), z_inside and r > 0)
-    if z_inside:
-        for chunk in range(3):
-            for r in range(1, dp):
-                for copy in part_sends(chunk, r):
-                    copy.wait_recv()
+    sums_done()
     sm_copy.wait()
 
 
 def finishing(
-    zr_t, zr_l, sums, rows_in_0, rows_in_1, rows_in_2, rows_in_3,
+    parts_t, parts_l, sums_in, rows_in_0, rows_in_1, rows_in_2, rows_in_3,
     rows_0, rows_1, rows_2, rows_3, att_t, out_t, exp_t, shr_t, att_l, out_l, exp_l, shr_l,
-    bias_t, off_t, vec_t, bias_l, off_l, vec_l, sems,
+    bias_t, off_t, vec_t, bias_l, off_l, vec_l,
+    zr_t, zr_l, sums, held_0, held_1, held_2, held_3, sems,
 ):
-    pairs = ((rows_in_0, rows_0), (rows_in_1, rows_1), (rows_in_2, rows_2), (rows_in_3, rows_3))
-    copies = [pltpu.make_async_copy(src, dst, sems.at[i]) for i, (src, dst) in enumerate(pairs)]
-    for copy in copies:
+    pairs = ((rows_in_0, held_0), (rows_in_1, held_1), (rows_in_2, held_2), (rows_in_3, held_3))
+    pairs += ((parts_t, zr_t), (parts_l, zr_l), (sums_in, sums))
+    loads = [pltpu.make_async_copy(src, dst, sems.at[i]) for i, (src, dst) in enumerate(pairs)]
+    for copy in loads:
         copy.start()
+    pairs = ((held_0, rows_0), (held_1, rows_1), (held_2, rows_2), (held_3, rows_3))
+    copies = [pltpu.make_async_copy(src, dst, sems.at[7 + i]) for i, (src, dst) in enumerate(pairs)]
+    for load, copy in zip(loads[:4], copies):
+        load.wait()
+        copy.start()
+    for load in loads[4:]:
+        load.wait()
     for zr, att, out, exp, shr in ((zr_t, att_t, out_t, exp_t, shr_t), (zr_l, att_l, out_l, exp_l, shr_l)):
         totals = []
         for chunk in range(3):
@@ -989,7 +1096,7 @@
     hs, ls = text_output.shape[2], layout_output.shape[2]
     ft, fl = text_expand.shape[2], layout_expand.shape[2]
     zt, zl = tw // dp, lw // dp
-    z_inside = dp <= 4 and zt % 16 == 0 and zl % 16 == 0
+    z_inside = dp == 4
 
     def shape(dims, dtype=bf16):
         return jax.ShapeDtypeStruct(dims, dtype)
@@ -1004,9 +1111,10 @@
     out_shape = row_shapes + [
         shape((16, SMALL), f32),
         shape((3, tw, tw)), shape((3, lw, lw)),
-        shape((3, dp, zt, tw)), shape((3, dp, zl, lw)),
+        shape((3, 4, tw // 4, tw)), shape((3, 4, lw // 4, lw)),
         shape((2, 3, 2, tw, tw)), shape((2, 3, 2, lw, lw)),
         shape((2, 3, tw // 2, tw)), shape((2, 3, lw // 2, lw)),
+        shape((2, 3, tw // 4, tw)), shape((2, 3, lw // 4, lw)),
         shape((3, 2, tw, tw)), shape((3, 2, lw, lw)),
         shape((3, tw, tw)), shape((3, lw, lw)),
         shape((2 * heads, tokens, tokens)),
@@ -1046,6 +1154,8 @@
         pltpu.VMEM((2, lw, lw), bf16),
         pltpu.VMEM((2, tw // 2, tw), bf16),
         pltpu.VMEM((2, lw // 2, lw), bf16),
+        pltpu.VMEM((2, tw // 4, tw), bf16),
+        pltpu.VMEM((2, lw // 4, lw), bf16),
         pltpu.VMEM((3, tw, tw), bf16),
         pltpu.VMEM((3, lw, lw), bf16),
         pltpu.VMEM((2, 2, 16, SMALL), f32),
@@ -1054,8 +1164,9 @@
         pltpu.VMEM((3, 16, SMALL), f32),
         dma((2, 2, 17)), dma((17, 2)), dma((2, 17, 2)), dma((3,)), dma((4, 5)), dma((8,)), dma((8,)),
         dma((4, 3)), dma((2, 2)), dma((2,)),
-        dma((2, 3, 2, 3)), dma((2, 3, 2)), dma((2, 3, 2)), dma((3, 2, 2, 2)), dma((3, 2)), dma((3, 2)),
-        dma((3, 2, 4)), dma((3, 2, 4)), dma((2, 3)), dma((2, 3, 4)), dma((2, 4)),
+        dma((2, 3, 2)), dma((2, 3, 2)), dma((2, 3, 2, 2)), dma((2, 3, 2, 2)), dma((2, 3, 2)), dma((2, 3, 2)),
+        dma((3, 2, 3, 2)), dma((3, 2)), dma((3, 2)), dma((3, 2, 2, 2)), dma((3, 4, 2)),
+        dma((2, 3)), dma((2, 3)), dma((3, 2, 2, 3)),
         dma((2, 2)), dma((4,)), dma((3,)), dma((3,)), dma((1,)),
     ]
     results = pl.pallas_call(
@@ -1092,10 +1203,13 @@
     ) = pl.pallas_call(
         finishing,
         out_shape=final_shapes,
-        in_specs=[vmem] * 3 + [hbm] * 4,
+        in_specs=[hbm] * 7,
         out_specs=[hbm] * 4 + [vmem] * 14,
-        scratch_shapes=[dma((4,))],
-        compiler_params=pltpu.CompilerParams(vmem_limit_bytes=32 * 1024 * 1024),
+        scratch_shapes=[
+            pltpu.VMEM(parts_t.shape, bf16), pltpu.VMEM(parts_l.shape, bf16), pltpu.VMEM((16, SMALL), f32),
+            *(pltpu.VMEM(rows.shape, bf16) for rows in row_shapes), dma((11,)),
+        ],
+        compiler_params=pltpu.CompilerParams(vmem_limit_bytes=62 * 1024 * 1024),
     )(parts_t, parts_l, sums, *row_results)
     return (
         text_out[None],

time: 326 us -> 284 us (0.87)
  Pallas kernels: 311 us -> 279 us
  local copies, waits for them, and re-layouts: 7.91 us -> 0 us
    pallas_call x1, Pallas kernels: 308 us -> 273 us  [local(): pl.pallas_call(functools.partial(kernel, dp, z_inside), out_shape=out_sha...]
    unnamed x14 -> x0, local copies, waits for them, and re-layouts: 7.91 us -> none
where the time goes in v1:
time: 284 us; the launch traced here: 280 us
  Pallas kernels  279 us (98%)
    pallas_call x1, Pallas kernels, local(): pl.pallas_call(functools.partial(kernel, dp, z_inside), out_shape=out_sha...  273 us

profile of v1, /device:TPU:0, one launch (start us, length us, event | category | flops | bytes accessed | tf_op | source)
XLA Modules:
  0.0 279.9 jit_solution(17891350292243181488)
XLA Ops:
  0.7 273.5 %shard_map.322 = (bf16[2,256,768]{2,1,0:T(8,128)(2,1)}, bf16[2,192,256]{2,1,0:T(8,128)(2,1)}, bf16[2,256,768]{2,1,0:T(8,128)(2,1)}, bf16[2,192,256]{2,1,0:T(8,12...) custom-call(bf16[2,256,768]{2,1,0:T(8,128)(2,1)} %text_in.1, ...), custom_call_target="tpu_custom_call" | custom-call | tf_op jit(solution)/shard_map/pallas_call | solution.py:1172
  274.1 5.6 %shard_map.323 = (bf16[2,256,768]{2,1,0:T(8,128)(2,1)}, bf16[2,192,256]{2,1,0:T(8,128)(2,1)}, bf16[2,256,768]{2,1,0:T(8,128)(2,1)}, bf16[2,192,256]{2,1,0:T(8,12...) custom-call(bf16[3,4,192,768]{3,2,1,0:T(8,128)(2,1)} %get-tuple-elem, ...), custom_call_target="tpu_custom_call" | custom-call | tf_op jit(solution)/shard_map/pallas_call | solution.py:1203

commit v2 on v1

--- a/solution.py
+++ b/solution.py
@@ -48,12 +48,12 @@
     text_in, lay_in, text_cot, lay_cot, att_t, out_t, exp_t, shr_t, att_l, out_l, exp_l, shr_l,
     bias_t, bias_l, off_t, off_l, vec_t, vec_l, lengths,
     text_out, lay_out, text_back, lay_back, sm_out,
-    zs_t, zs_l, zr_t, zr_l, gb_t, gb_l, rz_t, rz_l, r1_t, r1_l, r2_t, r2_l, ro_t, ro_l, p_keep,
+    zs_t, zs_l, zr_t, zr_l, zh_t, zh_l, gb_t, gb_l, rz_t, rz_l, rh_t, rh_l, r1_t, r1_l, r2_t, r2_l, ro_t, ro_l, p_keep,
     w_t, w_l, small, vecs, own_small, own_vec, key_bias, rows_t, rows_l, x_fm, qkv_t, qkv_l, probs,
     ctx_t, ctx_l, xh1, n1b, xh2, act, gp, stats, acc, exs, exr, tmpb, g_fm, dup, dqkv, cols,
     stg_t, stg_l, zv_t, zv_l, tv_t, tv_l, fv_t, fv_l, smsg, srec, ssum, szr,
     ag_recv, ag_own, ag_fwd, vec_sem, row_sem, ex_send, ex_recv, out_sem, stg_sem, p_sem,
-    rz_send, rz_recv, s1_send, d_send, r1_recv, s2_send, s2_recv, so_send, so_recv, z_send, z_recv,
+    rz_send, rz_recv, s1_send, d_send, r1_recv, s2_send, s2_recv, so_send, so_recv, z_send, z_recv, zh_recv,
     zv_sem, tv_sem, fv_sem,
     sm_send, sm_recv, sz_send, sz_recv, so_sem,
 ):
@@ -100,6 +100,11 @@
         for copy in copies:
             copy.wait()
 
+    barrier = pltpu.get_barrier_semaphore()
+    peers = [(1 - c, d, t)] + [(k, d, other) for other in (t1, t2, t3) for k in range(2)] + [(c, z, t) for z in z_peers]
+    for peer in peers:
+        pl.semaphore_signal(barrier, inc=1, device_id=peer, device_id_type=MESH)
+
     own_vec[...] = jnp.zeros(own_vec.shape, f32)
     own_vec[0:1, 0:hid_t] = off_t[...].astype(f32)
     own_vec[0:1, hid_t : hid_t + hid_l] = off_l[...].astype(f32)
@@ -110,11 +115,6 @@
     own_small[...] = own_vec[...].astype(bf16)
     own_vec[0:6, 0:tw] = vec_t[...].astype(f32)
     own_vec[0:6, tw:width] = vec_l[...].astype(f32)
-
-    barrier = pltpu.get_barrier_semaphore()
-    peers = [(1 - c, d, t)] + [(k, d, other) for other in (t1, t2, t3) for k in range(2)] + [(c, z, t) for z in z_peers]
-    for peer in peers:
-        pl.semaphore_signal(barrier, inc=1, device_id=peer, device_id_type=MESH)
     pl.semaphore_wait(barrier, len(peers))
     other = (1 - c, d, t)
 
@@ -232,12 +232,16 @@
         local_copy(own_vec, vecs.at[c], vec_sem.at[0]),
         remote(own_vec, vecs.at[c], vec_sem.at[1], vec_sem.at[2], other),
     ]
-    start(vec_copies)
 
     @pl.when(c == 0)
     def _():
-        for p in all_pieces:
-            start([own_first(p), own_local(p)])
+        start([own_first(p) for p in all_pieces])
+
+    start(vec_copies)
+
+    @pl.when(c == 0)
+    def _():
+        start([own_local(p) for p in all_pieces])
 
     @pl.when(c == 1)
     def _():
@@ -472,9 +476,7 @@
             need(1, 0)
             load_columns(1)
         else:
-            send_rows(0, 0, out_pair, x_fm.at[1])
-            second_norm(1, 3, tmpb)
-            send_rows(1, 0, out_pair, tmpb)
+            second_norm(1, 3, dup.at[0])
 
     def grad_store(layer, chunk, s):
         return [
@@ -497,14 +499,19 @@
     def quarters(first, count, size):
         return at(first * size, count * size)
 
-    def first_sends(layer, chunk):
+    def first_sends(layer, chunk, core):
         copies = []
         for g, (gb, rz, r1, r2, ro, zs, zr, zv, tv, fv, w, size) in enumerate(groups):
-            for i, rows in enumerate((quarters(far, 2, size), quarters(near + c, 1, size))):
+            if layer == 1:
+                parts = [pl.ds(0, 4 * size) if core else quarters(far, 2, size)]
+            else:
+                parts = [quarters(far, 2, size), quarters(near + core, 1, size)]
+            for i, rows in enumerate(parts):
                 copies.append(
                     remote(
-                        gb.at[layer, chunk, 1 - c, rows], r2.at[chunk, c, rows],
-                        s1_send.at[layer, chunk, g, i], s2_recv.at[chunk, c, i, g], (layer, d, tx),
+                        gb.at[layer, chunk, 1 - core, rows], r2.at[chunk, core, rows],
+                        s1_send.at[layer, chunk, g, i], s2_recv.at[chunk, core, i, g],
+                        (layer, d, t2 if core else t1),
                     )
                 )
         return copies
@@ -524,21 +531,34 @@
             for g, (gb, rz, *_, size) in enumerate(groups)
         ]
 
+    def diagonal_sends(layer, chunk):
+        copies = []
+        for g, (gb, rz, r1, *_, size) in enumerate(groups):
+            if layer == 1:
+                parts = [(quarters(near, 2, size), (rh_t, rh_l)[g].at[chunk], (0, d, t2))]
+            else:
+                parts = [(quarters(near + i, 1, size), r1.at[chunk], (1 - i, d, (t1, t2)[i])) for i in range(2)]
+            for i, (rows, dest, device) in enumerate(parts):
+                copies.append(
+                    remote(
+                        gb.at[layer, chunk, 1, rows], dest,
+                        d_send.at[layer, chunk, g, i], r1_recv.at[layer, chunk, g], device,
+                    )
+                )
+        return copies
+
+    def on(core, task, *args):
+        @pl.when(c == core)
+        def _():
+            task(*args)
+
     def grads_go(layer, chunk):
         for s in range(2):
             wait(grad_store(layer, chunk, s))
-
-        @pl.when(c == 1)
-        def _():
-            start(pair_sends(layer, chunk))
-
+        on(1, lambda: start(pair_sends(layer, chunk) + first_sends(layer, chunk, 1)))
+        on(0, lambda: start(first_sends(layer, chunk, 0)))
         if layer == 1:
-
-            @pl.when(c == 0)
-            def _():
-                start(own_sends(chunk))
-
-        start(first_sends(layer, chunk))
+            on(0, lambda: start(own_sends(chunk)))
 
     def pair_loads(layer, chunk):
         copies = []
@@ -553,18 +573,6 @@
             for g, (gb, rz, r1, r2, ro, zs, zr, zv, tv, fv, w, size) in enumerate(groups)
         ]
 
-    def diagonal_sends(layer, chunk):
-        copies = []
-        for g, (gb, rz, r1, *_, size) in enumerate(groups):
-            for i, device in enumerate(((1, d, t1), (0, d, t2))):
-                copies.append(
-                    remote(
-                        gb.at[layer, chunk, 1, quarters(near + i, 1, size)], r1.at[layer, chunk],
-                        d_send.at[layer, chunk, g, i], r1_recv.at[layer, chunk, g], device,
-                    )
-                )
-        return copies
-
     def pair_load(layer, chunk):
         @pl.when(c == 1)
         def _():
@@ -586,40 +594,52 @@
             wait(pair_stores(layer, chunk))
             start(diagonal_sends(layer, chunk))
 
-    def waiting(gb, layer, chunk, size):
-        return gb.at[layer, chunk, 1 - c, quarters(near + 1 - c, 1, size)]
+    def transit_parts(layer, chunk):
+        parts = []
+        for g, (gb, rz, r1, r2, ro, zs, zr, zv, tv, fv, w, size) in enumerate(groups):
+            if layer == 1:
+                parts.append((gb.at[1, chunk, 1, quarters(near, 2, size)], (rh_t, rh_l)[g].at[chunk], zv, zv_sem))
+            else:
+                rows = quarters(near + 1 - c, 1, size)
+                parts.append((gb.at[0, chunk, 1 - c, rows], r1.at[chunk], tv, tv_sem))
+        return parts
 
     def transit_loads(layer, chunk):
         copies = []
-        for g, (gb, rz, r1, r2, ro, zs, zr, zv, tv, fv, w, size) in enumerate(groups):
-            copies.append(local_copy(waiting(gb, layer, chunk, size), tv.at[0], tv_sem.at[g, 0]))
-            copies.append(local_copy(r1.at[layer, chunk], tv.at[1], tv_sem.at[g, 1]))
+        for g, (mine, come, held, sem) in enumerate(transit_parts(layer, chunk)):
+            copies.append(local_copy(mine, held.at[0], sem.at[g, 0]))
+            copies.append(local_copy(come, held.at[1], sem.at[g, 1]))
         return copies
 
     def transit_stores(layer, chunk):
         return [
-            local_copy(tv.at[0], waiting(gb, layer, chunk, size), tv_sem.at[g, 2])
-            for g, (gb, rz, r1, r2, ro, zs, zr, zv, tv, fv, w, size) in enumerate(groups)
+            local_copy(held.at[0], mine, sem.at[g, 2])
+            for g, (mine, come, held, sem) in enumerate(transit_parts(layer, chunk))
         ]
 
     def second_sends(layer, chunk):
-        return [
-            remote(
-                waiting(gb, layer, chunk, size), r2.at[chunk, c, quarters(near + 1 - c, 1, size)],
-                s2_send.at[layer, chunk, g], s2_recv.at[chunk, c, 2, g], (layer, d, tx),
+        copies = []
+        for g, (mine, come, held, sem) in enumerate(transit_parts(layer, chunk)):
+            gb, rz, r1, r2, *_, size = groups[g]
+            if layer == 1:
+                dest, device = r2.at[chunk, 0, quarters(near, 2, size)], (1, d, t1)
+            else:
+                dest, device = r2.at[chunk, c, quarters(near + 1 - c, 1, size)], (0, d, tx)
+            way, which = (0, 1) if layer == 1 else (c, 2)
+            copies.append(
+                remote(mine, dest, s2_send.at[layer, chunk, g], s2_recv.at[chunk, way, which, g], device)
             )
-            for g, (gb, rz, r1, r2, *_, size) in enumerate(groups)
-        ]
+        return copies
 
     def transit_load(layer, chunk):
-        for g, (gb, rz, r1, *_) in enumerate(groups):
-            landed(r1.at[layer, chunk], r1_recv.at[layer, chunk, g])
+        for g, (mine, come, held, sem) in enumerate(transit_parts(layer, chunk)):
+            landed(come, r1_recv.at[layer, chunk, g])
         start(transit_loads(layer, chunk))
 
     def transit_add(layer, chunk):
         wait(transit_loads(layer, chunk))
-        for tv in (tv_t, tv_l):
-            tv[0] = (tv[0].astype(f32) + tv[1].astype(f32)).astype(bf16)
+        for mine, come, held, sem in transit_parts(layer, chunk):
+            held[0] = (held[0].astype(f32) + held[1].astype(f32)).astype(bf16)
         start(transit_stores(layer, chunk))
 
     def transit_send(layer, chunk):
@@ -627,48 +647,67 @@
         start(second_sends(layer, chunk))
 
     def final_loads(layer, chunk, stage):
-        first = near if stage else far
         copies = []
         for g, (gb, rz, r1, r2, ro, zs, zr, zv, tv, fv, w, size) in enumerate(groups):
-            rows = quarters(first, 2, size)
+            rows = quarters(near if stage else far, 2, size)
             own = ro.at[chunk, rows] if layer == 1 else gb.at[0, chunk, 0, rows]
-            places = (w.at[1, 0, chunk, rows], w.at[1, 1, chunk, rows], fv.at[chunk, rows])
-            for i, src in enumerate((own, r2.at[chunk, 0, rows], r2.at[chunk, 1, rows])):
-                copies.append(local_copy(src, places[i], fv_sem.at[chunk, stage, g, i]))
+            terms = [
+                (own, w.at[1, 0, chunk, rows]),
+                (r2.at[chunk, 0, rows], w.at[1, 1, chunk, rows]),
+                (r2.at[chunk, 1, rows], fv.at[chunk, rows]),
+            ]
+            if z_inside and stage == 1:
+                terms.append(((zh_t, zh_l)[g].at[chunk], fv.at[chunk, quarters(far, 2, size)]))
+            for i, (src, dst) in enumerate(terms):
+                copies.append(local_copy(src, dst, fv_sem.at[chunk, stage, g, i]))
         return copies
 
     def final_load(layer, chunk, stage):
         @pl.when(c == layer)
         def _():
             for g, (gb, rz, r1, r2, ro, zs, zr, zv, tv, fv, w, size) in enumerate(groups):
-                for way in range(2):
-                    if stage == 0:
-                        landed(r2.at[chunk, way, quarters(far, 2, size)], s2_recv.at[chunk, way, 0, g])
-                    else:
-                        landed(r2.at[chunk, way, quarters(near + way, 1, size)], s2_recv.at[chunk, way, 1, g])
-                        landed(r2.at[chunk, way, quarters(near + 1 - way, 1, size)], s2_recv.at[chunk, way, 2, g])
+
+                def came(way, first, count, which):
+                    landed(r2.at[chunk, way, quarters(first, count, size)], s2_recv.at[chunk, way, which, g])
+
                 if layer == 1 and stage == 0:
+                    came(0, far, 2, 0)
+                    came(1, 0, 4, 0)
                     landed(ro.at[chunk], so_recv.at[chunk, g])
+                elif layer == 1:
+                    came(0, near, 2, 1)
+                else:
+                    for way in range(2):
+                        if stage == 0:
+                            came(way, far, 2, 0)
+                        else:
+                            came(way, near + way, 1, 1)
+                            came(way, near + 1 - way, 1, 2)
+                if z_inside and stage == 1:
+                    landed((zh_t, zh_l)[g].at[chunk], zh_recv.at[chunk, g])
             start(final_loads(layer, chunk, stage))
 
-    def z_send_of(chunk, stage, i, g):
+    def half_send(chunk, g):
         gb, rz, r1, r2, ro, zs, zr, zv, tv, fv, w, size = groups[g]
-        j = (near if stage else far) + i
-        return j, w.at[1, 0, chunk, quarters(j, 1, size)], zr.at[chunk, d]
-
-    def z_remote(chunk, stage, i, g):
-        j, piece, dest = z_send_of(chunk, stage, i, g)
-        return remote(piece, dest, z_send.at[chunk, stage, i, g], z_recv.at[chunk, d, g], (c, j, t))
+        return remote(
+            w.at[1, 0, chunk, quarters(far, 2, size)], (zh_t, zh_l)[g].at[chunk],
+            z_send.at[chunk, 0, g], zh_recv.at[chunk, g], (c, dz, t),
+        )
+
+    def quarter_send(chunk, i, g, away):
+        gb, rz, r1, r2, ro, zs, zr, zv, tv, fv, w, size = groups[g]
+        piece, dest = w.at[1, 0, chunk, quarters(near + i, 1, size)], zr.at[chunk, lax.div(d, 2)]
+        recv = z_recv.at[chunk, lax.div(d, 2), g]
+        if away:
+            return remote(piece, dest, z_send.at[chunk, 1 + i, g], recv, (c, near + i, t))
+        return local_copy(piece, dest, recv)
 
     def sum_stores(chunk, stage):
-        first = near if stage else far
-        return [
-            local_copy(
-                w.at[1, 0, chunk, quarters(first, 2, size)], zs.at[chunk, quarters(first, 2, size)],
-                z_send.at[chunk, stage, 0, g],
-            )
-            for g, (gb, rz, r1, r2, ro, zs, zr, zv, tv, fv, w, size) in enumerate(groups)
-        ]
+        copies = []
+        for g, (gb, rz, r1, r2, ro, zs, zr, zv, tv, fv, w, size) in enumerate(groups):
+            rows = quarters(near if stage else far, 2, size)
+            copies.append(local_copy(w.at[1, 0, chunk, rows], zs.at[chunk, rows], z_send.at[chunk, stage, g]))
+        return copies
 
     def final_add(layer, chunk, stage):
         @pl.when(c == layer)
@@ -677,43 +716,40 @@
             for gb, rz, r1, r2, ro, zs, zr, zv, tv, fv, w, size in groups:
                 rows = quarters(near if stage else far, 2, size)
                 total = w[1, 0, chunk, rows].astype(f32) + w[1, 1, chunk, rows].astype(f32)
-                w[1, 0, chunk, rows] = (total + fv[chunk, rows].astype(f32)).astype(bf16)
+                total = total + fv[chunk, rows].astype(f32)
+                if z_inside and stage == 1:
+                    total = total + fv[chunk, quarters(far, 2, size)].astype(f32)
+                w[1, 0, chunk, rows] = total.astype(bf16)
             if not z_inside:
                 start(sum_stores(chunk, stage))
-                return
-            for i in range(2):
-                for g in range(2):
-                    j, piece, dest = z_send_of(chunk, stage, i, g)
-
-                    @pl.when(j != d)
+            elif stage == 0:
+                start([half_send(chunk, g) for g in range(2)])
+            else:
+                for i in range(2):
+
+                    @pl.when(near + i != d)
                     def _():
-                        z_remote(chunk, stage, i, g).start()
-
-                    @pl.when(j == d)
+                        start([quarter_send(chunk, i, g, True) for g in range(2)])
+
+                    @pl.when(near + i == d)
                     def _():
-                        local_copy(piece, dest, z_recv.at[chunk, d, g]).start()
-
-    def final(layer, chunk, stage):
-        final_load(layer, chunk, stage)
-        final_add(layer, chunk, stage)
+                        start([quarter_send(chunk, i, g, False) for g in range(2)])
 
     def sums_done():
         for chunk in range(3):
-            for stage in range(2):
-                if not z_inside:
-                    wait(sum_stores(chunk, stage))
-                    continue
+            if not z_inside:
+                wait(sum_stores(chunk, 0) + sum_stores(chunk, 1))
+                continue
+            for g in range(2):
+                half_send(chunk, g).wait_send()
                 for i in range(2):
-                    for g in range(2):
-
-                        @pl.when(z_send_of(chunk, stage, i, g)[0] != d)
-                        def _():
-                            z_remote(chunk, stage, i, g).wait_send()
-
-            if z_inside:
-                for j in range(dp):
-                    for g in range(2):
-                        landed(groups[g][6].at[chunk, j], z_recv.at[chunk, j, g])
+
+                    @pl.when(near + i != d)
+                    def _():
+                        quarter_send(chunk, i, g, True).wait_send()
+
+                for k in range(2):
+                    landed(groups[g][6].at[chunk, k], z_recv.at[chunk, k, g])
 
     def small_sends(layer):
         zero = [remote(smsg.at[layer, 1], srec.at[0], sm_send.at[layer, 0], sm_recv.at[0], (layer, d, t1))]
@@ -782,6 +818,8 @@
                 g_fm[pl.ds(first, size), lanes] = grad.astype(bf16)
 
         loop(0, blocks, block)
+
+    def norm_sums(layer, which):
         vector_sum(layer, 3 * which + 1, row_sums(exs))
         vector_sum(layer, 3 * which + 2, row_sums(g_fm))
         vector_sum(layer, 3 * which, row_sums(tmpb))
@@ -897,23 +935,19 @@
         (1, "heads 1"): [(Z[2], 1, 2), (Z[0], 1, 1)],
         (1, "heads 2"): [(Z[1], 1, 1)],
         (1, "attend grads"): [(Z[2], 1, 1)],
-        (1, "swap"): [(T[0], 1, 2)],
-        (1, "swapped"): [(T[1], 1, 2)],
-        (1, "finished"): [(T[2], 1, 2)],
-        (0, "begin"): [(gather_sent,), (T[0], 1, 1)],
-        (0, "second norm"): [(T[1], 1, 1), (Z[0], 1, 0), (F[0], 1, 2, 0)],
-        (0, "shrink grads"): [(T[2], 1, 1), (Z[1], 1, 0)],
-        (0, "ffn"): [(Z[2], 1, 0), (F[1], 1, 2, 0)],
-        (0, "expand grads"): [(T[0], 1, 0), (F[0], 1, 2, 1)],
-        (0, "ffn swap"): [(F[1], 1, 2, 1)],
-        (0, "first norm"): [(T[1], 1, 0), (F[0], 1, 1, 0), (Z[0], 0, 2)],
-        (0, "context"): [(T[2], 1, 0)],
-        (0, "heads 0"): [(Z[1], 0, 2), (F[1], 1, 1, 0), (F[0], 1, 1, 1)],
-        (0, "heads 1"): [(Z[2], 0, 2), (Z[0], 0, 1), (F[1], 1, 1, 1)],
-        (0, "heads 2"): [(Z[1], 0, 1), (T[0], 0, 2), (F[0], 1, 0, 0)],
-        (0, "attend grads"): [(Z[2], 0, 1), (T[1], 0, 2), (F[1], 1, 0, 0)],
-        (0, "swap"): [(T[2], 0, 2), (F[0], 1, 0, 1)],
-        (0, "finished"): [(F[1], 1, 0, 1)],
+        (0, "begin"): [(gather_sent,), (F[0], 1, 2, 0)],
+        (0, "second norm"): [(F[1], 1, 2, 0)],
+        (0, "shrink grads"): [(Z[0], 1, 0), (F[0], 1, 1, 0)],
+        (0, "ffn"): [(Z[1], 1, 0)],
+        (0, "expand grads"): [(Z[2], 1, 0), (on, 0, T[0], 1, 2)],
+        (0, "ffn swap"): [(on, 0, T[1], 1, 2), (F[1], 1, 1, 0)],
+        (0, "first norm"): [(on, 0, T[2], 1, 2), (on, 0, T[0], 1, 1), (Z[0], 0, 2)],
+        (0, "context"): [(on, 0, T[1], 1, 1), (Z[1], 0, 2)],
+        (0, "heads 0"): [(on, 0, T[2], 1, 1), (Z[2], 0, 2)],
+        (0, "heads 2"): [(Z[0], 0, 1)],
+        (0, "attend grads"): [(Z[1], 0, 1)],
+        (0, "swap"): [(Z[2], 0, 1), (F[0], 1, 0, 0)],
+        (0, "finished"): [(F[1], 1, 0, 0)],
     }
 
     for layer in (1, 0):
@@ -930,9 +964,13 @@
         point("second norm")
         for s in range(2):
             shrink_grads(layer, s)
+        norm_sums(layer, 1)
+        grads_go(layer, 2)
+        if not last:
+            send_rows(0, 0, out_pair, x_fm.at[1])
+            send_rows(1, 0, out_pair, dup.at[0])
         point("shrink grads")
         ffn_backward(layer)
-        grads_go(layer, 2)
         point("ffn")
         for s in range(2):
             expand_grads(layer, s)
@@ -946,6 +984,7 @@
         point("ffn swap")
         swap.wait()
         norm_backward(layer, 0, xh1, functools.partial(first_grad, n))
+        norm_sums(layer, 0)
         point("first norm")
         if last:
             p_load.wait()
@@ -982,13 +1021,25 @@
         finish_rows(layer, 0, out_pair)
         stage_rows(layer, g_fm)
 
-    run(
-        *((step, 0, 1) for step in T), *((step, 0, 0) for step in Z),
-        (final, 0, 2, 0), (final, 0, 2, 1), (small_total, 1), (final, 0, 1, 0),
-        *((step, 0, 0) for step in T),
-    )
-    start(rows_out(2, *back_pair))
-    run((small_total, 0), (final, 0, 1, 1), (final, 0, 0, 0), (final, 0, 0, 1))
+    def transit(layer, chunk):
+        run(*((step, layer, chunk) for step in T))
+
+    def final(layer, chunk, stage):
+        run(*((step, layer, chunk, stage) for step in F))
+
+    @pl.when(c == 0)
+    def _():
+        run((final, 0, 2, 0), (transit, 1, 0), (final, 0, 1, 0), (transit, 0, 2), (final, 0, 0, 0))
+        run((transit, 0, 1), (transit, 0, 0))
+        start(rows_out(2, *back_pair))
+        run((final, 0, 2, 1), (final, 0, 1, 1), (small_total, 0), (final, 0, 0, 1))
+
+    @pl.when(c == 1)
+    def _():
+        run(*((step, 0, 0) for step in Z), (transit, 0, 2), (final, 1, 2, 1), (transit, 0, 1), (final, 1, 1, 1))
+        run((small_total, 1), (transit, 0, 0))
+        start(rows_out(2, *back_pair))
+        run((final, 1, 0, 1))
 
     for copy in small_z():
         copy.wait()
@@ -1007,16 +1058,16 @@
                 for copy in smalls[core]:
                     copy.wait_send()
                 for chunk in range(3):
+                    copies = first_sends(layer, chunk, core)
                     if core == 1:
-                        for copy in pair_sends(layer, chunk) + diagonal_sends(layer, chunk):
-                            copy.wait_send()
+                        copies += pair_sends(layer, chunk) + diagonal_sends(layer, chunk)
                     elif layer == 1:
-                        for copy in own_sends(chunk):
-                            copy.wait_send()
-
-        for chunk in range(3):
-            for copy in first_sends(layer, chunk) + second_sends(layer, chunk):
-                copy.wait_send()
+                        copies += own_sends(chunk)
+                    if core == 0 or layer == 0:
+                        copies += second_sends(layer, chunk)
+                    for copy in copies:
+                        copy.wait_send()
+
     sums_done()
     sm_copy.wait()
 
@@ -1111,10 +1162,10 @@
     out_shape = row_shapes + [
         shape((16, SMALL), f32),
         shape((3, tw, tw)), shape((3, lw, lw)),
-        shape((3, 4, tw // 4, tw)), shape((3, 4, lw // 4, lw)),
+        shape((3, 2, tw // 4, tw)), shape((3, 2, lw // 4, lw)), shape((3, tw // 2, tw)), shape((3, lw // 2, lw)),
         shape((2, 3, 2, tw, tw)), shape((2, 3, 2, lw, lw)),
-        shape((2, 3, tw // 2, tw)), shape((2, 3, lw // 2, lw)),
-        shape((2, 3, tw // 4, tw)), shape((2, 3, lw // 4, lw)),
+        shape((2, 3, tw // 2, tw)), shape((2, 3, lw // 2, lw)), shape((3, tw // 2, tw)), shape((3, lw // 2, lw)),
+        shape((3, tw // 4, tw)), shape((3, lw // 4, lw)),
         shape((3, 2, tw, tw)), shape((3, 2, lw, lw)),
         shape((3, tw, tw)), shape((3, lw, lw)),
         shape((2 * heads, tokens, tokens)),
@@ -1165,8 +1216,8 @@
         dma((2, 2, 17)), dma((17, 2)), dma((2, 17, 2)), dma((3,)), dma((4, 5)), dma((8,)), dma((8,)),
         dma((4, 3)), dma((2, 2)), dma((2,)),
         dma((2, 3, 2)), dma((2, 3, 2)), dma((2, 3, 2, 2)), dma((2, 3, 2, 2)), dma((2, 3, 2)), dma((2, 3, 2)),
-        dma((3, 2, 3, 2)), dma((3, 2)), dma((3, 2)), dma((3, 2, 2, 2)), dma((3, 4, 2)),
-        dma((2, 3)), dma((2, 3)), dma((3, 2, 2, 3)),
+        dma((3, 2, 3, 2)), dma((3, 2)), dma((3, 2)), dma((3, 3, 2)), dma((3, 2, 2)), dma((3, 2)),
+        dma((2, 3)), dma((2, 3)), dma((3, 2, 2, 4)),
         dma((2, 2)), dma((4,)), dma((3,)), dma((3,)), dma((1,)),
     ]
     results = pl.pallas_call(

time: 284 us -> 268 us (0.944)
  the two profiles are of different devices: /device:TPU:0 before, /device:TPU:24 now
where the time goes in v2:
time: 268 us; the launch traced here: 264 us
  Pallas kernels  263 us (98%)
    pallas_call x1, Pallas kernels, local(): pl.pallas_call(functools.partial(kernel, dp, z_inside), out_shape=out_sha...  259 us

profile of v2, /device:TPU:24, one launch (start us, length us, event | category | flops | bytes accessed | tf_op | source)
XLA Modules:
  0.0 263.8 jit_solution(538023614763230146)
XLA Ops:
  0.7 258.9 %shard_map.322 = (bf16[2,256,768]{2,1,0:T(8,128)(2,1)}, bf16[2,192,256]{2,1,0:T(8,128)(2,1)}, bf16[2,256,768]{2,1,0:T(8,128)(2,1)}, bf16[2,192,256]{2,1,0:T(8,12...) custom-call(bf16[2,256,768]{2,1,0:T(8,128)(2,1)} %text_in.1, ...), custom_call_target="tpu_custom_call" | custom-call | tf_op jit(solution)/shard_map/pallas_call | solution.py:1223
  259.6 4.0 %shard_map.323 = (bf16[2,256,768]{2,1,0:T(8,128)(2,1)}, bf16[2,192,256]{2,1,0:T(8,128)(2,1)}, bf16[2,256,768]{2,1,0:T(8,128)(2,1)}, bf16[2,192,256]{2,1,0:T(8,12...) custom-call(bf16[3,2,192,768]{3,2,1,0:T(8,128)(2,1)} %get-tuple-elem, ...), custom_call_target="tpu_custom_call" | custom-call | tf_op jit(solution)/shard_map/pallas_call | solution.py:1254
